TPU v7x, 32 devices: a whole 2x2x4 slice. The times are simulated.
32 devices in a mesh: rad: 4 (over y, x), azi: 8 (over z, core).
Axes of the slice: x: 2, y: 2, z: 4, core: 2. Of those that a mesh axis runs over, the one named last changes fastest.
Arguments:
- tokens: bfloat16 [32, 128, 8, 512], P('rad', 'azi'), may hold values from -6 to 6
- cotangent: bfloat16 [32, 128, 8, 512], P('rad', 'azi'), may hold values from -6 to 6
- ln_gain: float32 [512], replicated, may hold values from 0.5 to 1.5
- qkv_weight: bfloat16 [512, 1536], P('azi'), may hold values from -2 to 2
- out_weight: bfloat16 [512, 512], P('azi'), may hold values from -0.25 to 0.25
- shear_offset: int32 [1], replicated, may hold values from 0 to 127
- window_shift: int32 [3], replicated, may hold values from 1 to 7, as said below
Outputs:
- block_out: bfloat16 [32, 128, 8, 512], P('rad', 'azi')
- grad_tokens: bfloat16 [32, 128, 8, 512], P('rad', 'azi')
- grad_qkv: float32 [512, 1536], P('azi')
- grad_out: float32 [512, 512], P('azi')
- grad_gain: float32 [512], replicated
Inputs may be any that keep to these rules, and one draw needn't show every extreme that they name: `window_shift`: the radial entry lies in 1 to 3; the azimuthal and vertical entries lie in 1 to 7, and one of these two equals 7.
All inputs are finite; a program needn't handle non-finite values.
Results may differ from a plain program's by a relative error of at most 0.025.
Values may be sent and summed in bfloat16 or wider, within the bound.
No kernel may reach another device: no remote copies, remote signals or barrier semaphores. Data moves between devices by JAX's collectives and lax.ppermute only.
A program may use at most 192 MiB of HBM per device.

v0:
```python
import jax
import jax.numpy as jnp
from jax import lax
from jax.experimental import pallas as pl
from jax.experimental.pallas import tpu as pltpu
from jax.sharding import PartitionSpec as P

HEADS = 16
HD = 32
WR = 4
WA = 8
WZ = 8
LANES = 128
LOG2E = 1.4426950408889634

EPS = 1e-05
NT = (((1,), (1,)), ((), ()))
TN = (((0,), (0,)), ((), ()))


def mm(a, b, dims=(((1,), (0,)), ((), ()))):
    return lax.dot_general(a, b, dims, preferred_element_type=jnp.float32)


def block_kernel(info_ref, *refs):
    x_ref, g_ref, side_ref, main_ref, next_ref, gain_ref = refs[:6]
    weight_refs, refs = refs[6:-20], refs[-20:]
    y_ref, dx_ref, strip_ref, rim_ref, gw_ref, gg_ref, f_s, w_ref = refs[:8]
    x_s, g_s, xhat_s, qkv_s, da_s, att_s, dqkv_s = refs[8:15]
    hid_all, att_all, gs_all, dqkv_all, gain_s = refs[15:20]
    step = pl.program_id(0)
    steps = pl.num_programs(0)
    rows, cols, depth, width = x_ref.shape
    rim_rows, rim_cols = strip_ref.shape[1], rim_ref.shape[2]
    grid_a = cols // WA
    tokens = WR * WA * WZ
    first_row, first_col, wrap_col = info_ref[0], info_ref[1], info_ref[2]

    @pl.when(step == 0)
    def _():
        f_s[0] = x_ref[...]
        f_s[1] = g_ref[...]

        def put_strip(n, carry):
            row, col = n // cols, lax.rem(n, cols)
            for f in range(2):
                f_s[f, row, col] = jnp.where(
                    col < wrap_col, next_ref[f, row, col], main_ref[f, row, col]
                )
            return carry

        def put_side(col, carry):
            def put(row, carry):
                for f in range(2):
                    f_s[f, row, col] = side_ref[f, row, col]
                return carry

            return lax.fori_loop(first_row, rows, put, carry)

        lax.fori_loop(0, first_row * cols, put_strip, 0)
        lax.fori_loop(0, first_col, put_side, 0)
        splits = len(weight_refs) // 2
        n_z, share, _ = weight_refs[0].shape
        for n, ref in enumerate(weight_refs):
            core = info_ref[4] if n < splits else 1 - info_ref[4]
            part = lax.rem(info_ref[5] + n % splits, splits)
            for d in range(n_z):
                z = lax.rem(info_ref[3] + d, n_z)
                at = ((z * 2 + core) * splits + part) * share
                w_ref[pl.ds(pl.multiple_of(at, share), share), :] = ref[d]

    places = []
    for k in range(WR):
        row = lax.rem(first_row + (step // grid_a) * WR + k, rows)
        start = jnp.where(row < first_row, wrap_col, first_col) + (step % grid_a) * WA
        for m in range(WA):
            places.append((row, lax.rem(start + m, cols)))
    for at, (row, col) in enumerate(places):
        x_s[at * WZ:(at + 1) * WZ, :] = f_s[0, row, col].astype(jnp.float32)
        g_s[at * WZ:(at + 1) * WZ, :] = f_s[1, row, col].astype(jnp.float32)
    x = x_s[...]
    gs = g_s[...].astype(jnp.bfloat16)
    gain = gain_ref[...]
    centred = x - jnp.mean(x, axis=1, keepdims=True)
    inv = lax.rsqrt(jnp.mean(centred * centred, axis=1, keepdims=True) + EPS)
    xhat = centred * inv
    xhat_s[...] = xhat
    hidden = (xhat * gain).astype(jnp.bfloat16)
    scaling = HD ** (-0.5)
    q_scaled = mm(hidden, w_ref[:, :width]) * (scaling * LOG2E)
    qkv_s[:, :width] = q_scaled.astype(jnp.bfloat16)
    qkv_s[:, width:] = mm(hidden, w_ref[:, width: 3 * width]).astype(jnp.bfloat16)
    da_s[...] = mm(gs, w_ref[:, 3 * width:], NT).astype(jnp.bfloat16)
    lane = lax.broadcasted_iota(jnp.int32, (1, LANES), 1)
    per_group = LANES // HD

    at_once = width // LANES
    heads = at_once * per_group

    def some_groups(step, carry):
        loaded, taken = {}, {}

        def load(g):
            base = pl.multiple_of((step * at_once + g) * LANES, LANES)
            q = qkv_s[:, pl.ds(base, LANES)]
            k = qkv_s[:, pl.ds(width + base, LANES)]
            v = qkv_s[:, pl.ds(2 * width + base, LANES)]
            da = da_s[:, pl.ds(base, LANES)]
            loaded[g] = q, k, v, da
            k_t = k.astype(jnp.float32).T.astype(jnp.bfloat16)
            v_t = v.astype(jnp.float32).T.astype(jnp.bfloat16)
            taken[g] = k_t, v_t, da.astype(jnp.float32).T

        zeros = jnp.zeros((tokens, LANES), jnp.float32)
        dv, dk = [zeros] * at_once, [zeros] * at_once
        att_t, dq_t = [[] for _ in range(at_once)], [[] for _ in range(at_once)]

        def products(n):
            g, h = n // per_group, n % per_group
            if g not in loaded:
                load(g)
            q, k, v, da = loaded[g]
            mine = (lane >= h * HD) & (lane < (h + 1) * HD)
            mask = jnp.where(mine, 1.0, 0.0).astype(jnp.bfloat16)
            qm = q * mask
            dam = da * mask
            return qm, dam, mm(k, qm, NT), mm(v, dam, NT)

        def forward(n, ready):
            g, h = n // per_group, n % per_group
            qm, dam, s, dp = ready
            _, v_t, da_t = taken[g]
            mine_t = slice(h * HD, (h + 1) * HD)
            e = jnp.exp2(s - jnp.max(s, axis=0, keepdims=True))
            p = e * (1.0 / jnp.sum(e, axis=0, keepdims=True))
            p_low = p.astype(jnp.bfloat16)
            att = mm(v_t[mine_t], p_low)
            att_t[g].append(att)
            dv[g] += mm(p_low, dam)
            return p, dp, jnp.sum(att * da_t[mine_t], axis=0, keepdims=True), qm

        def backward(n, softened):
            g, h = n // per_group, n % per_group
            p, dp, delta, qm = softened
            ds = (p * (dp - delta)).astype(jnp.bfloat16)
            dk[g] += mm(ds, qm)
            dq_t[g].append(mm(taken[g][0][h * HD:(h + 1) * HD], ds))

        ready, softened = products(0), None
        for n in range(heads):
            now = ready
            if n + 1 < heads:
                ready = products(n + 1)
            before, softened = softened, forward(n, now)
            if before is not None:
                backward(n - 1, before)
        backward(heads - 1, softened)
        for g in range(at_once):
            base = pl.multiple_of((step * at_once + g) * LANES, LANES)
            att_s[:, pl.ds(base, LANES)] = (
                jnp.concatenate(att_t[g], axis=0).T.astype(jnp.bfloat16)
            )
            dqkv_s[:, pl.ds(base, LANES)] = (
                jnp.concatenate(dq_t[g], axis=0).T * scaling
            ).astype(jnp.bfloat16)
            dqkv_s[:, pl.ds(width + base, LANES)] = (dk[g] * (1.0 / LOG2E)).astype(jnp.bfloat16)
            dqkv_s[:, pl.ds(2 * width + base, LANES)] = dv[g].astype(jnp.bfloat16)
        return carry

    lax.fori_loop(0, width // LANES // at_once, some_groups, 0)
    att = att_s[...]
    d_qkv = dqkv_s[...]
    d_hidden = mm(d_qkv, w_ref[:, : 3 * width], NT)
    xhat = xhat_s[...]
    term_gain = jnp.sum(d_hidden * xhat, axis=0, keepdims=True)
    d_normed = d_hidden * gain
    y = x_s[...] + mm(att, w_ref[:, 3 * width:])
    dx = g_s[...] + inv * (
        d_normed
        - jnp.mean(d_normed, axis=1, keepdims=True)
        - xhat * jnp.mean(d_normed * xhat, axis=1, keepdims=True)
    )
    for at, (row, col) in enumerate(places):
        y_ref[row, col] = y[at * WZ:(at + 1) * WZ].astype(jnp.bfloat16)
        dx_ref[row, col] = dx[at * WZ:(at + 1) * WZ].astype(jnp.bfloat16)
    here = pl.ds(pl.multiple_of(step * tokens, tokens), tokens)
    hid_all[here, :] = hidden
    att_all[here, :] = att
    gs_all[here, :] = gs
    dqkv_all[here, :] = d_qkv

    @pl.when(step == 0)
    def _():
        gain_s[...] = jnp.zeros_like(gain_s)

    gain_s[...] += term_gain

    @pl.when(step == steps - 1)
    def _():
        for f, ref in enumerate((y_ref, dx_ref)):
            strip_ref[f] = ref[:rim_rows]
            rim_ref[f] = ref[:, :rim_cols]
        g_qkv = mm(hid_all[...], dqkv_all[...], TN).astype(jnp.bfloat16)
        g_out = mm(att_all[...], gs_all[...], TN).astype(jnp.bfloat16)
        gg_ref[...] = gain_s[...]
        if len(gw_ref.shape) == 2:
            gw_ref[:, : 3 * width] = g_qkv
            gw_ref[:, 3 * width:] = g_out
        else:
            cores, n_rad, n_z, part, _ = gw_ref.shape
            extra = jnp.concatenate(
                [gain_s[:, n * LANES:(n + 1) * LANES] for n in range(width // LANES)]
                + [jnp.zeros((part - width // LANES, LANES), jnp.float32)],
                axis=0,
            ).astype(jnp.bfloat16)
            for n in range(cores * n_rad * n_z):
                z, core, i = n // n_rad // cores, n // n_rad % cores, n % n_rad
                here = gw_ref.at[core, i, z]
                here[:, : 3 * width] = g_qkv[n * part:(n + 1) * part]
                here[:, 3 * width: 4 * width] = g_out[n * part:(n + 1) * part]
                here[:, 4 * width:] = extra


def block_pass(info, x, g, side, main, following, gain, weights, term_shape):
    rows, cols, depth, width = x.shape
    tokens = WR * WA * WZ
    number = rows * cols * depth

    def whole(shape):
        return pl.BlockSpec(shape, lambda i, info: (0,) * len(shape))

    bf, f32 = jnp.bfloat16, jnp.float32
    strip_shape = (2, WR - 1, cols, depth, width)
    rim_shape = (2, rows, WA - 1, depth, width)
    ins = (x, g, side, main, following, gain) + tuple(weights)
    outs = [
        (x.shape, bf), (x.shape, bf), (strip_shape, bf), (rim_shape, bf),
        (term_shape, bf), ((1, width), f32),
    ]
    return pl.pallas_call(
        block_kernel,
        grid_spec=pltpu.PrefetchScalarGridSpec(
            num_scalar_prefetch=1,
            grid=(number // tokens,),
            in_specs=[whole(array.shape) for array in ins],
            out_specs=[whole(shape) for shape, _ in outs],
            scratch_shapes=[
                pltpu.VMEM((2,) + x.shape, bf),
                pltpu.VMEM((width, 4 * width), bf),
                pltpu.VMEM((tokens, width), f32),
                pltpu.VMEM((tokens, width), f32),
                pltpu.VMEM((tokens, width), f32),
                pltpu.VMEM((tokens, 3 * width), bf),
                pltpu.VMEM((tokens, width), bf),
                pltpu.VMEM((tokens, width), bf),
                pltpu.VMEM((tokens, 3 * width), bf),
                pltpu.VMEM((number, width), bf),
                pltpu.VMEM((number, width), bf),
                pltpu.VMEM((number, width), bf),
                pltpu.VMEM((number, 3 * width), bf),
                pltpu.VMEM((1, width), f32),
            ],
        ),
        out_shape=[jax.ShapeDtypeStruct(shape, kind) for shape, kind in outs],
        compiler_params=pltpu.CompilerParams(vmem_limit_bytes=56 * 1024 * 1024),
        cost_estimate=pl.CostEstimate(
            flops=number * width * width * 24, bytes_accessed=16 * 2 ** 20, transcendentals=0
        ),
        name="block_pass",
    )(info, *ins)


BOTH = ("rad", "azi")


def route(pairs, array, back):
    n_azi = lax.axis_size("azi")
    flat = [(a[0] * n_azi + a[1], b[0] * n_azi + b[1]) for a, b in pairs]
    return lax.ppermute(array, BOTH, [(t, s) if back else (s, t) for s, t in flat])


def strip_routes(hops, back):
    n_rad, n_azi = lax.axis_size("rad"), lax.axis_size("azi")
    azi = range(n_azi)
    near = [((i + 1, j), (i, j)) for i in range(n_rad - 1) for j in azi]
    wrap = [((0, (j + hops) % n_azi), (n_rad - 1, j)) for j in azi]
    return near, wrap


def beside(array, back):
    n_rad, n_azi = lax.axis_size("rad"), lax.axis_size("azi")
    pairs = [((i, (j + 1) % n_azi), (i, j)) for i in range(n_rad) for j in range(n_azi)]
    return route(pairs, array, back)


def over_switch(body, arrays, shift_rad, hops):
    n_azi = lax.axis_size("azi")
    sizes = range(1, WR) if n_azi <= 16 else [WR - 1]
    branches = [body(rows, n) for rows in sizes for n in range(n_azi)]
    index = (shift_rad - 1) * n_azi + hops if len(sizes) > 1 else hops
    return lax.switch(index, branches, *arrays)


def full_rows(array):
    missing = WR - 1 - array.shape[1]
    return jnp.pad(array, ((0, 0), (0, missing), (0, 0), (0, 0), (0, 0)))


def radial_strip(strip, shift_rad, hops, back):
    def body(rows, hops):
        def send(strip):
            near, wrap = strip_routes(hops, back)
            return full_rows(route(near + wrap, strip[:, :rows], back))

        return send

    return over_switch(body, (strip,), shift_rad, hops)


def permuted(array, axis, target):
    count = lax.axis_size(axis)
    return lax.ppermute(array, axis, [(n, target(n)) for n in range(count)])


def scatter_sum(pieces, index, send, hold=lambda arrays: arrays):
    count = pieces.shape[0]
    if count > 4 and count % 2 == 0:
        half = count // 2
        halves = pieces.reshape((2, half) + pieces.shape[1:])
        upper = index // half
        kept = lax.dynamic_index_in_dim(halves, upper, 0, keepdims=False)
        given = lax.dynamic_index_in_dim(halves, 1 - upper, 0, keepdims=False)
        got = send(given, lambda n: (n + half) % count)
        kept = (kept.astype(jnp.float32) + got.astype(jnp.float32)).astype(pieces.dtype)
        return scatter_sum(
            kept,
            index % half,
            lambda array, to: send(array, lambda n: n // half * half + to(n % half)),
            hold,
        )
    total = lax.dynamic_index_in_dim(pieces, index, 0, keepdims=False).astype(jnp.float32)
    arrived = []
    for d in range(1, count):
        given = lax.dynamic_index_in_dim(pieces, (index + d) % count, 0, keepdims=False)
        arrived.append(send(given, lambda n: (n + d) % count))
    for got in hold(arrived):
        total = total + got.astype(jnp.float32)
    return total.astype(pieces.dtype)


def over_core(cores):
    return lambda array, to: permuted(
        array, "azi", lambda n: n // cores * cores + to(n % cores)
    )


def over_z(cores):
    return lambda array, to: permuted(
        array, "azi", lambda n: to(n // cores) * cores + n % cores
    )


def over_rad(array, to):
    return permuted(array, "rad", to)


def fetch_all(strip, side, shard, shift_rad, hops, cores):
    n_rad, n_z = lax.axis_size("rad"), lax.axis_size("azi") // cores
    first_z = first_part = 0
    split = n_z <= 4 and n_rad % 2 == 0
    if split:
        first_z = lax.axis_index("azi") // cores
        first_part = lax.axis_index("rad") % 2
        share = shard.shape[0] // 2
        half = lax.dynamic_slice_in_dim(shard, first_part * share, share, 0)
        mine = [half] + [over_z(cores)(half, lambda n: (n - d) % n_z) for d in range(1, n_z)]
    else:
        groups = [list(range(core, n_z * cores, cores)) for core in range(cores)]
        mine = [lax.all_gather(shard, "azi", axis=0, axis_index_groups=groups)]
    side = beside(side, False)
    main = radial_strip(strip, shift_rad, hops, False)
    main, side, mine = lax.optimization_barrier((main, side, mine))
    following = beside(main, False)
    if split:
        mine = jnp.stack(mine)
        mine = [mine, over_rad(mine, lambda n: n // 2 * 2 + (n + 1) % 2)]
    weights = mine + [over_core(cores)(part, lambda n: (n + 1) % cores) for part in mine]
    return main, following, side, weights, first_z, first_part


def on_device(tokens, cotangent, ln_gain, qkv_weight, out_weight, shear_offset, window_shift):
    rows_dev, cols_dev, depth, width = tokens.shape
    assert depth == WZ
    number = rows_dev * cols_dev * depth
    n_rad = lax.axis_size("rad")
    n_azi = lax.axis_size("azi")
    at_rad = lax.axis_index("rad")
    total_cols = cols_dev * n_azi
    rim_rows, rim_cols = WR - 1, WA - 1
    shift_rad = window_shift[0]
    shift_azi = window_shift[1]
    offset = shear_offset[0]
    amount = (offset + shift_azi) % total_cols
    hops = amount // cols_dev
    cores = 2
    assert n_azi % cores == 0
    shard = jnp.concatenate([qkv_weight, out_weight], axis=1)
    side = jnp.stack([tokens[:, :rim_cols], cotangent[:, :rim_cols]])
    strip = jnp.stack([tokens[:rim_rows], cotangent[:rim_rows]])
    main, following, side, weights, first_z, first_part = fetch_all(
        strip, side, shard, shift_rad, hops, cores
    )
    last = at_rad == n_rad - 1
    wrap_col = jnp.where(last, amount % cols_dev, shift_azi)
    at_core = lax.axis_index("azi") % cores
    info = [shift_rad, shift_azi, wrap_col, first_z, at_core, first_part]
    info = jnp.stack([jnp.asarray(value, jnp.int32) for value in info])
    part_rows = width // n_azi // n_rad
    placed = part_rows % 16 == 0
    pieces_shape = (cores, n_rad, n_azi // cores, part_rows, 4 * width + LANES)
    y, dx, strip, side, term, gain = block_pass(
        info, tokens, cotangent, side, main, following, ln_gain.reshape(1, width), weights,
        pieces_shape if placed else (width, 4 * width),
    )
    following = beside(strip, True)
    following, side = lax.optimization_barrier((following, side))
    side = beside(side, True)
    col = jnp.arange(cols_dev, dtype=jnp.int32).reshape(1, 1, cols_dev, 1, 1)
    if placed:
        at_azi = lax.axis_index("azi")
        term = scatter_sum(term, at_azi % cores, over_core(cores))
        strip_back = []

        def beside_strip(arrays):
            arrays, back, beside_it = lax.optimization_barrier(
                (arrays, radial_strip(strip, shift_rad, hops, True), side)
            )
            strip_back.extend((back, beside_it))
            return arrays

        term = scatter_sum(term, at_rad, over_rad)
        following, term = lax.optimization_barrier((following, term))
        strip = jnp.where(col < wrap_col, following, strip)
        mine = scatter_sum(term, at_azi // cores, over_z(cores), beside_strip)
        strip, side = strip_back
    else:
        strip = jnp.where(col < wrap_col, following, strip)
        strip = radial_strip(strip, shift_rad, hops, True)
    if placed:
        others = [over_rad(mine, lambda n: (n - d) % n_rad) for d in range(1, n_rad)]
        share = jnp.roll(jnp.stack([mine] + others), at_rad, axis=0)
    col = jnp.arange(rim_cols, dtype=jnp.int32).reshape(1, rim_cols, 1, 1)
    row = jnp.arange(rim_rows, dtype=jnp.int32).reshape(rim_rows, 1, 1, 1)

    def finish(array, strip, side):
        edge = jnp.where(col < shift_azi, side, array[:, :rim_cols])
        array = lax.dynamic_update_slice(array, edge, (0, 0, 0, 0))
        edge = jnp.where(row < shift_rad, strip, array[:rim_rows])
        return lax.dynamic_update_slice(array, edge, (0, 0, 0, 0))

    block_out = finish(y, strip[0], side[0])
    grad_tokens = finish(dx, strip[1], side[1])
    if placed:
        gain = share[0, :, 4 * width:].reshape(-1)[:width].astype(jnp.float32)
        share = share[:, :, : 4 * width].reshape(n_rad * part_rows, 4 * width)
    else:
        gain = lax.psum(gain[0], BOTH)
        share = lax.psum_scatter(term, "azi", scatter_dimension=0, tiled=True)
        share = lax.psum(share, "rad")
    share = share.astype(jnp.float32)
    factor = float(number * n_rad * n_azi) ** (-0.5)
    grad_qkv = share[:, : 3 * width] * factor
    grad_out = share[:, 3 * width :] * factor
    return (block_out, grad_tokens, grad_qkv, grad_out, gain * factor)


def solution(mesh):
    in_specs = (
        P("rad", "azi", None, None),
        P("rad", "azi", None, None),
        P(),
        P("azi", None),
        P("azi", None),
        P(),
        P(),
    )
    out_specs = (
        P("rad", "azi", None, None),
        P("rad", "azi", None, None),
        P("azi", None),
        P("azi", None),
        P(),
    )
    return jax.shard_map(
        on_device, mesh=mesh, in_specs=in_specs, out_specs=out_specs, check_vma=False
    )
```

profile of v0, /device:TPU:0, one launch (start us, length us, event | category | flops | bytes accessed | tf_op | source)
XLA Modules:
  0.0 161.6 jit_solution(5255128451004990442)
XLA Ops:
  0.6 1.2 slice_bitcast_fusion
  1.9 0.1 pad_maximum_fusion
  2.0 4.5 %collective-permute-start.48 = (bf16[2,8,7,8,512]{4,3,2,1,0:T(8,128)(2,1)S(1)}, bf16[2,8,7,8,512]{4,3,2,1,0:T(8,128)(2,1)S(1)}, u32[]{:S(2)}, u32[]{:S(2)}) collective-permute-start(bf16[2,8,7,8,512]{4,3,2,1,0:T(8,128)(2,1)S(1)} %pad_maximum_fusion), channel_id=1, source_target_pairs={{1,0},{2,1},{3,2},{4,3},{5,4},{6,5},{7,6},{0,7},{9,8},{10,9},{11,1... | collective-permute-start | bytes 2752520 | tf_op jit(solution)/shard_map/ppermute | solution.py:279
  6.6 1.4 collective-permute-start.49
  7.9 1.0 collective-permute-start.51
  9.6 0.6 fusion.13
  11.5 1.2 slice_bitcast_fusion.2
  12.7 0.1 pad_maximum_fusion.1
  12.8 30.1 %conditional.2 = (bf16[2,3,16,8,512]{4,3,2,1,0:T(8,128)(2,1)}) conditional(s32[]{:T(128)} %clamp.4, bf16[2,3,16,8,512]{4,3,2,1,0:T(8,128)(2,1)S(1)} %pad_maximum_fusion.1, bf16[2,3,16,8,512]{4,3,2,1,0:T(8,128)(2,1)S(1)} %pad_maximum_fusion.1, bf16[2,3,16,8,512]{4,3,2,1,0:T(8,128)(2,1)S(1)} %pad_maximum_fusion.1, ...), branch_computations={%region_0.1_spmd, %region_1.2_spmd, %region_2.3_spmd, %region_3.4_... | conditional | bytes 4456498 | solution.py:301
  12.8 4.7 %collective-permute-start.18 = (bf16[2,3,16,8,512]{4,3,2,1,0:T(8,128)(2,1)S(1)}, bf16[2,3,16,8,512]{4,3,2,1,0:T(8,128)(2,1)}, u32[]{:S(2)}, u32[]{:S(2)}) collective-permute-start(bf16[2,3,16,8,512]{4,3,2,1,0:T(8,128)(2,1)S(1)} %param.18), channel_id=1, source_target_pairs={{8,0},{9,1},{10,2},{11,3},{12,4},{13,5},{14,6},{15,7},{16,8},{17,9... | collective-permute-start | bytes 2359304 | tf_op jit(solution)/shard_map/cond/branch_18_fun/ppermute | solution.py:279
  17.6 25.3 %collective-permute-done.18 = bf16[2,3,16,8,512]{4,3,2,1,0:T(8,128)(2,1)} collective-permute-done((bf16[2,3,16,8,512]{4,3,2,1,0:T(8,128)(2,1)S(1)}, bf16[2,3,16,8,512]{4,3,2,1,0:T(8,128)(2,1)}, u32[]{:S(2)}, u32[]{:S(2)}) %collective-permute-start.18) | collective-permute-done | bytes 786464 | tf_op jit(solution)/shard_map/cond/branch_18_fun/ppermute | solution.py:279
  43.1 0.2 collective-permute-start.52
  43.3 0.5 collective-permute-start.54
  43.8 8.4 %collective-permute-done.53.refs_7_ = bf16[4,32,2048]{2,1,0:T(8,128)(2,1)S(1)} collective-permute-done((bf16[4,32,2048]{2,1,0:T(8,128)(2,1)S(1)}, bf16[4,32,2048]{2,1,0:T(8,128)(2,1)S(1)}, u32[]{:S(2)}, u32[]{:S(2)}) %collective-permute-start.53) | collective-permute-done | bytes 524320 | tf_op jit(solution)/shard_map/ppermute | solution.py:322
  52.9 0.6 stack.137.info_ref
  53.5 0.8 collective-permute-done.55.refs_9_
  54.3 0.3 copy-done.11
  54.6 32.4 %block_pass.1 = (bf16[8,16,8,512]{3,2,1,0:T(8,128)(2,1)}, bf16[8,16,8,512]{3,2,1,0:T(8,128)(2,1)}, bf16[2,3,16,8,512]{4,3,2,1,0:T(8,128)(2,1)}, bf16[2,8,7,8,512...) custom-call(s32[6]{0:T(128)} %stack.137.info_ref, bf16[8,16,8,512]{3,2,1,0:T(8,128)(2,1)} %refs_0_.1, ...), custom_call_target="tpu_custom_call" | custom-call | flops 6442450944 | bytes 16777216 | tf_op jit(solution)/shard_map/block_pass/pallas_call | solution.py:240
  87.0 1.5 dynamic-slice_bitcast_fusion
  88.5 11.8 %collective-permute-start.57 = (bf16[4,4,16,2176]{3,2,1,0:T(8,128)(2,1)S(1)}, bf16[4,4,16,2176]{3,2,1,0:T(8,128)(2,1)}, u32[]{:S(2)}, u32[]{:S(2)}) collective-permute-start(bf16[4,4,16,2176]{3,2,1,0:T(8,128)(2,1)S(1)} %dynamic-slice_bitcast_fusion), channel_id=1, source_target_pairs={{0,1},{1,0},{2,3},{3,2},{4,5},{5,4},{6,7},{7,6},{8,9},{9,8},{10,11... | collective-permute-start | bytes 3342344 | tf_op jit(solution)/shard_map/ppermute | solution.py:322
  100.3 0.1 collective-permute-start.56
  100.4 2.8 %collective-permute-done.57 = bf16[4,4,16,2176]{3,2,1,0:T(8,128)(2,1)} collective-permute-done((bf16[4,4,16,2176]{3,2,1,0:T(8,128)(2,1)S(1)}, bf16[4,4,16,2176]{3,2,1,0:T(8,128)(2,1)}, u32[]{:S(2)}, u32[]{:S(2)}) %collective-permute-start.57) | collective-permute-done | bytes 1114144 | tf_op jit(solution)/shard_map/ppermute | solution.py:322
  103.2 1.5 fusion
  104.7 0.9 dynamic-slice_bitcast_fusion.3
  105.6 1.8 %collective-permute-start.58 = (bf16[4,16,2176]{2,1,0:T(8,128)(2,1)}, bf16[4,16,2176]{2,1,0:T(8,128)(2,1)}, u32[]{:S(2)}, u32[]{:S(2)}) collective-permute-start(bf16[4,16,2176]{2,1,0:T(8,128)(2,1)} %get-tuple-element.145), channel_id=1, source_target_pairs={{0,8},{8,16},{16,24},{24,0},{1,9},{9,17},{17,25},{25,1},{2,10},{10... | collective-permute-start | bytes 835592 | tf_op jit(solution)/shard_map/ppermute | solution.py:322
  107.4 1.5 collective-permute-start.60
  108.8 0.6 iota_compare_fusion.2
  109.5 0.7 iota_compare_fusion
  110.1 3.7 %collective-permute-done.56 = bf16[2,3,16,8,512]{4,3,2,1,0:T(8,128)(2,1)} collective-permute-done((bf16[2,3,16,8,512]{4,3,2,1,0:T(8,128)(2,1)}, bf16[2,3,16,8,512]{4,3,2,1,0:T(8,128)(2,1)}, u32[]{:S(2)}, u32[]{:S(2)}) %collective-permute-start.56) | collective-permute-done | bytes 786464 | tf_op jit(solution)/shard_map/ppermute | solution.py:279
  113.8 2.5 %collective-permute-done.58 = bf16[4,16,2176]{2,1,0:T(8,128)(2,1)} collective-permute-done((bf16[4,16,2176]{2,1,0:T(8,128)(2,1)}, bf16[4,16,2176]{2,1,0:T(8,128)(2,1)}, u32[]{:S(2)}, u32[]{:S(2)}) %collective-permute-start.58) | collective-permute-done | bytes 278560 | tf_op jit(solution)/shard_map/ppermute | solution.py:322
  116.3 5.4 %collective-permute-done.59 = bf16[4,16,2176]{2,1,0:T(8,128)(2,1)} collective-permute-done((bf16[4,16,2176]{2,1,0:T(8,128)(2,1)}, bf16[4,16,2176]{2,1,0:T(8,128)(2,1)}, u32[]{:S(2)}, u32[]{:S(2)}) %collective-permute-start.59) | collective-permute-done | bytes 278560 | tf_op jit(solution)/shard_map/ppermute | solution.py:322
  121.7 1.3 fusion.3
  123.0 0.7 dynamic-slice_bitcast_fusion.4
  123.7 2.4 %collective-permute-start.61 = (bf16[16,2176]{1,0:T(8,128)(2,1)}, bf16[16,2176]{1,0:T(8,128)(2,1)S(1)}, u32[]{:S(2)}, u32[]{:S(2)}) collective-permute-start(bf16[16,2176]{1,0:T(8,128)(2,1)} %get-tuple-element.154), channel_id=1, source_target_pairs={{0,2},{1,3},{2,4},{3,5},{4,6},{5,7},{6,0},{7,1},{8,10},{9,11},{10,... | collective-permute-start | bytes 208904 | tf_op jit(solution)/shard_map/ppermute | solution.py:322
  126.1 2.5 %collective-permute-start.63 = (bf16[16,2176]{1,0:T(8,128)(2,1)S(1)}, bf16[16,2176]{1,0:T(8,128)(2,1)}, u32[]{:S(2)}, u32[]{:S(2)}) collective-permute-start(bf16[16,2176]{1,0:T(8,128)(2,1)S(1)} %get-tuple-element.152), channel_id=1, source_target_pairs={{0,6},{1,7},{2,0},{3,1},{4,2},{5,3},{6,4},{7,5},{8,14},{9,15},{10,... | collective-permute-start | bytes 208904 | tf_op jit(solution)/shard_map/ppermute | solution.py:322
  128.6 1.3 broadcast_select_fusion
  129.9 22.7 %conditional.3 = (bf16[2,3,16,8,512]{4,3,2,1,0:T(8,128)(2,1)}) conditional(s32[]{:T(128)} %clamp.4, bf16[2,3,16,8,512]{4,3,2,1,0:T(8,128)(2,1)S(1)} %broadcast_select_fusion, bf16[2,3,16,8,512]{4,3,2,1,0:T(8,128)(2,1)S(1)} %broadcast_select_fusion, bf16[2,3,16,8,512]{4,3,2,1,0:T(8,128)(2,1)S(1)} %broadcast_select_fusion, ...), branch_computations={%region_24.25_spmd, %region_25.26_spmd, %region_26.27_spmd, %regio... | conditional | bytes 4456498 | solution.py:301
  130.0 1.4 collective-permute-start.42
  131.3 21.3 %collective-permute-done.42 = bf16[2,3,16,8,512]{4,3,2,1,0:T(8,128)(2,1)} collective-permute-done((bf16[2,3,16,8,512]{4,3,2,1,0:T(8,128)(2,1)S(1)}, bf16[2,3,16,8,512]{4,3,2,1,0:T(8,128)(2,1)}, u32[]{:S(2)}, u32[]{:S(2)}) %collective-permute-start.42) | collective-permute-done | bytes 786464 | tf_op jit(solution)/shard_map/cond/branch_18_fun/ppermute | solution.py:279
  152.6 0.9 bitcast_dynamic-update-slice_fusion.6
  153.7 1.9 %collective-permute-start.67 = (bf16[16,2176]{1,0:T(8,128)(2,1)S(1)}, bf16[16,2176]{1,0:T(8,128)(2,1)S(1)}, u32[]{:S(2)}, u32[]{:S(2)}) collective-permute-start(bf16[16,2176]{1,0:T(8,128)(2,1)S(1)} %get-tuple-element.144), channel_id=1, source_target_pairs={{0,8},{8,16},{16,24},{24,0},{1,9},{9,17},{17,25},{25,1},{2,10},{10... | collective-permute-start | bytes 208904 | tf_op jit(solution)/shard_map/ppermute | solution.py:322
  155.6 0.4 fusion.4
  156.1 1.5 fusion.6
  157.6 0.3 collective-permute-done.65
  158.0 1.4 collective-permute-done.67
  159.6 0.8 slice_multiply_fusion
  160.3 0.7 slice_multiply_fusion.1
  161.0 0.6 multiply_bitcast_fusion
  (59 shorter events, 0.6 us)
Async XLA Ops:
  1.9 4.7 %copy-start.7 = (bf16[64,1536]{1,0:T(8,128)(2,1)S(1)}, bf16[64,1536]{1,0:T(8,128)(2,1)}, u32[]{:S(2)}) copy-start(bf16[64,1536]{1,0:T(8,128)(2,1)} %param.58) | copy-start | bytes 589828
  1.9 4.7 %copy-start.8 = (bf16[64,512]{1,0:T(8,128)(2,1)S(1)}, bf16[64,512]{1,0:T(8,128)(2,1)}, u32[]{:S(2)}) copy-start(bf16[64,512]{1,0:T(8,128)(2,1)} %param.59) | copy-start | bytes 196612
  1.9 7.7 %copy-start.9 = (s32[3]{0:T(128)S(1)}, s32[3]{0:T(128)}, u32[]{:S(2)}) copy-start(s32[3]{0:T(128)} %param.61) | copy-start | bytes 40
  2.0 40.9 %collective-permute-start.48 = (bf16[2,8,7,8,512]{4,3,2,1,0:T(8,128)(2,1)S(1)}, bf16[2,8,7,8,512]{4,3,2,1,0:T(8,128)(2,1)S(1)}, u32[]{:S(2)}, u32[]{:S(2)}) collective-permute-start(bf16[2,8,7,8,512]{4,3,2,1,0:T(8,128)(2,1)S(1)} %pad_maximum_fusion), channel_id=1, source_target_pairs={{1,0},{2,1},{3,2},{4,3},{5,4},{6,5},{7,6},{0,7},{9,8},{10,9},{11,1... | collective-permute-start | bytes 2752520 | tf_op jit(solution)/shard_map/ppermute | solution.py:279
  6.6 36.3 %collective-permute-start.49 = (bf16[32,2048]{1,0:T(8,128)(2,1)S(1)}, bf16[32,2048]{1,0:T(8,128)(2,1)S(1)}, u32[]{:S(2)}, u32[]{:S(2)}) collective-permute-start(bf16[32,2048]{1,0:T(8,128)(2,1)S(1)} %fusion.11), channel_id=1, source_target_pairs={{0,6},{1,7},{2,0},{3,1},{4,2},{5,3},{6,4},{7,5},{8,14},{9,15},{10,... | collective-permute-start | bytes 393224 | tf_op jit(solution)/shard_map/ppermute | solution.py:322
  7.9 35.0 %collective-permute-start.50 = (bf16[32,2048]{1,0:T(8,128)(2,1)S(1)}, bf16[32,2048]{1,0:T(8,128)(2,1)S(1)}, u32[]{:S(2)}, u32[]{:S(2)}) collective-permute-start(bf16[32,2048]{1,0:T(8,128)(2,1)S(1)} %fusion.11), channel_id=1, source_target_pairs={{0,4},{1,5},{2,6},{3,7},{4,0},{5,1},{6,2},{7,3},{8,12},{9,13},{10,... | collective-permute-start | bytes 393224 | tf_op jit(solution)/shard_map/ppermute | solution.py:322
  7.9 35.0 %collective-permute-start.51 = (bf16[32,2048]{1,0:T(8,128)(2,1)S(1)}, bf16[32,2048]{1,0:T(8,128)(2,1)S(1)}, u32[]{:S(2)}, u32[]{:S(2)}) collective-permute-start(bf16[32,2048]{1,0:T(8,128)(2,1)S(1)} %fusion.11), channel_id=1, source_target_pairs={{0,2},{1,3},{2,4},{3,5},{4,6},{5,7},{6,0},{7,1},{8,10},{9,11},{10,... | collective-permute-start | bytes 393224 | tf_op jit(solution)/shard_map/ppermute | solution.py:322
  12.8 30.0 %collective-permute-start.18 = (bf16[2,3,16,8,512]{4,3,2,1,0:T(8,128)(2,1)S(1)}, bf16[2,3,16,8,512]{4,3,2,1,0:T(8,128)(2,1)}, u32[]{:S(2)}, u32[]{:S(2)}) collective-permute-start(bf16[2,3,16,8,512]{4,3,2,1,0:T(8,128)(2,1)S(1)} %param.18), channel_id=1, source_target_pairs={{8,0},{9,1},{10,2},{11,3},{12,4},{13,5},{14,6},{15,7},{16,8},{17,9... | collective-permute-start | bytes 2359304 | tf_op jit(solution)/shard_map/cond/branch_18_fun/ppermute | solution.py:279
  42.9 11.4 %copy-start.10 = (bf16[2,8,7,8,512]{4,3,2,1,0:T(8,128)(2,1)}, bf16[2,8,7,8,512]{4,3,2,1,0:T(8,128)(2,1)S(1)}, u32[]{:S(2)}) copy-start(bf16[2,8,7,8,512]{4,3,2,1,0:T(8,128)(2,1)S(1)} %collective-permute-done.48.refs_2_) | copy-start | bytes 2752516
  43.0 11.3 %copy-start.6 = (bf16[4,32,2048]{2,1,0:T(8,128)(2,1)}, bf16[4,32,2048]{2,1,0:T(8,128)(2,1)S(1)}, u32[]{:S(2)}) copy-start(bf16[4,32,2048]{2,1,0:T(8,128)(2,1)S(1)} %pad_maximum_fusion.2.refs_6_) | copy-start | bytes 1572868
  43.0 9.2 %collective-permute-start.53 = (bf16[4,32,2048]{2,1,0:T(8,128)(2,1)S(1)}, bf16[4,32,2048]{2,1,0:T(8,128)(2,1)S(1)}, u32[]{:S(2)}, u32[]{:S(2)}) collective-permute-start(bf16[4,32,2048]{2,1,0:T(8,128)(2,1)S(1)} %pad_maximum_fusion.2.refs_6_), channel_id=1, source_target_pairs={{0,8},{8,0},{16,24},{24,16},{1,9},{9,1},{17,25},{25,17},{2,10},{10... | collective-permute-start | bytes 1572872 | tf_op jit(solution)/shard_map/ppermute | solution.py:322
  43.1 10.4 %collective-permute-start.52 = (bf16[2,3,16,8,512]{4,3,2,1,0:T(8,128)(2,1)}, bf16[2,3,16,8,512]{4,3,2,1,0:T(8,128)(2,1)S(1)}, u32[]{:S(2)}, u32[]{:S(2)}) collective-permute-start(bf16[2,3,16,8,512]{4,3,2,1,0:T(8,128)(2,1)} %get-tuple-element.161.refs_3_), channel_id=1, source_target_pairs={{1,0},{2,1},{3,2},{4,3},{5,4},{6,5},{7,6},{0,7},{9,8},{10,9},{11,1... | collective-permute-start | bytes 2359304 | tf_op jit(solution)/shard_map/ppermute | solution.py:279
  43.3 10.2 %collective-permute-start.54 = (bf16[4,32,2048]{2,1,0:T(8,128)(2,1)S(1)}, bf16[4,32,2048]{2,1,0:T(8,128)(2,1)S(1)}, u32[]{:S(2)}, u32[]{:S(2)}) collective-permute-start(bf16[4,32,2048]{2,1,0:T(8,128)(2,1)S(1)} %pad_maximum_fusion.2.refs_6_), channel_id=1, source_target_pairs={{0,1},{1,0},{2,3},{3,2},{4,5},{5,4},{6,7},{7,6},{8,9},{9,8},{10,11... | collective-permute-start | bytes 1572872 | tf_op jit(solution)/shard_map/ppermute | solution.py:322
  52.2 2.1 %copy-start.12 = (bf16[4,32,2048]{2,1,0:T(8,128)(2,1)}, bf16[4,32,2048]{2,1,0:T(8,128)(2,1)S(1)}, u32[]{:S(2)}) copy-start(bf16[4,32,2048]{2,1,0:T(8,128)(2,1)S(1)} %collective-permute-done.53.refs_7_) | copy-start | bytes 1572868
  52.2 2.0 %collective-permute-start.55 = (bf16[4,32,2048]{2,1,0:T(8,128)(2,1)S(1)}, bf16[4,32,2048]{2,1,0:T(8,128)(2,1)}, u32[]{:S(2)}, u32[]{:S(2)}) collective-permute-start(bf16[4,32,2048]{2,1,0:T(8,128)(2,1)S(1)} %collective-permute-done.53.refs_7_), channel_id=1, source_target_pairs={{0,1},{1,0},{2,3},{3,2},{4,5},{5,4},{6,7},{7,6},{8,9},{9,8},{10,11... | collective-permute-start | bytes 1572872 | tf_op jit(solution)/shard_map/ppermute | solution.py:322
  53.5 0.8 copy-start.13
  53.5 1.1 copy-start.11
  87.0 16.2 %copy-start = (bf16[2,4,4,16,2176]{4,3,2,1,0:T(8,128)(2,1)S(1)}, bf16[2,4,4,16,2176]{4,3,2,1,0:T(8,128)(2,1)}, u32[]{:S(2)}) copy-start(bf16[2,4,4,16,2176]{4,3,2,1,0:T(8,128)(2,1)} %get-tuple-element.133) | copy-start | bytes 6684676
  88.5 14.7 %collective-permute-start.57 = (bf16[4,4,16,2176]{3,2,1,0:T(8,128)(2,1)S(1)}, bf16[4,4,16,2176]{3,2,1,0:T(8,128)(2,1)}, u32[]{:S(2)}, u32[]{:S(2)}) collective-permute-start(bf16[4,4,16,2176]{3,2,1,0:T(8,128)(2,1)S(1)} %dynamic-slice_bitcast_fusion), channel_id=1, source_target_pairs={{0,1},{1,0},{2,3},{3,2},{4,5},{5,4},{6,7},{7,6},{8,9},{9,8},{10,11... | collective-permute-start | bytes 3342344 | tf_op jit(solution)/shard_map/ppermute | solution.py:322
  100.3 13.5 %collective-permute-start.56 = (bf16[2,3,16,8,512]{4,3,2,1,0:T(8,128)(2,1)}, bf16[2,3,16,8,512]{4,3,2,1,0:T(8,128)(2,1)}, u32[]{:S(2)}, u32[]{:S(2)}) collective-permute-start(bf16[2,3,16,8,512]{4,3,2,1,0:T(8,128)(2,1)} %get-tuple-element.130), channel_id=1, source_target_pairs={{0,1},{1,2},{2,3},{3,4},{4,5},{5,6},{6,7},{7,0},{8,9},{9,10},{10,1... | collective-permute-start | bytes 2359304 | tf_op jit(solution)/shard_map/ppermute | solution.py:279
  105.6 23.0 %copy-start.1 = (bf16[2,3,16,8,512]{4,3,2,1,0:T(8,128)(2,1)S(1)}, bf16[2,3,16,8,512]{4,3,2,1,0:T(8,128)(2,1)}, u32[]{:S(2)}) copy-start(bf16[2,3,16,8,512]{4,3,2,1,0:T(8,128)(2,1)} %get-tuple-element.130) | copy-start | bytes 2359300
  105.6 10.7 %collective-permute-start.58 = (bf16[4,16,2176]{2,1,0:T(8,128)(2,1)}, bf16[4,16,2176]{2,1,0:T(8,128)(2,1)}, u32[]{:S(2)}, u32[]{:S(2)}) collective-permute-start(bf16[4,16,2176]{2,1,0:T(8,128)(2,1)} %get-tuple-element.145), channel_id=1, source_target_pairs={{0,8},{8,16},{16,24},{24,0},{1,9},{9,17},{17,25},{25,1},{2,10},{10... | collective-permute-start | bytes 835592 | tf_op jit(solution)/shard_map/ppermute | solution.py:322
  107.4 14.3 %collective-permute-start.59 = (bf16[4,16,2176]{2,1,0:T(8,128)(2,1)}, bf16[4,16,2176]{2,1,0:T(8,128)(2,1)}, u32[]{:S(2)}, u32[]{:S(2)}) collective-permute-start(bf16[4,16,2176]{2,1,0:T(8,128)(2,1)} %get-tuple-element.147), channel_id=1, source_target_pairs={{0,16},{8,24},{16,0},{24,8},{1,17},{9,25},{17,1},{25,9},{2,18},{10... | collective-permute-start | bytes 835592 | tf_op jit(solution)/shard_map/ppermute | solution.py:322
  107.4 14.3 %collective-permute-start.60 = (bf16[4,16,2176]{2,1,0:T(8,128)(2,1)S(1)}, bf16[4,16,2176]{2,1,0:T(8,128)(2,1)}, u32[]{:S(2)}, u32[]{:S(2)}) collective-permute-start(bf16[4,16,2176]{2,1,0:T(8,128)(2,1)S(1)} %get-tuple-element.146), channel_id=1, source_target_pairs={{0,24},{8,0},{16,8},{24,16},{1,25},{9,1},{17,9},{25,17},{2,26},{10... | collective-permute-start | bytes 835592 | tf_op jit(solution)/shard_map/ppermute | solution.py:322
  113.8 38.8 %collective-permute-start.64 = (bf16[2,8,7,8,512]{4,3,2,1,0:T(8,128)(2,1)}, bf16[2,8,7,8,512]{4,3,2,1,0:T(8,128)(2,1)S(1)}, u32[]{:S(2)}, u32[]{:S(2)}) collective-permute-start(bf16[2,8,7,8,512]{4,3,2,1,0:T(8,128)(2,1)} %get-tuple-element.136), channel_id=1, source_target_pairs={{0,1},{1,2},{2,3},{3,4},{4,5},{5,6},{6,7},{7,0},{8,9},{9,10},{10,1... | collective-permute-start | bytes 2752520 | tf_op jit(solution)/shard_map/ppermute | solution.py:279
  123.7 28.9 %collective-permute-start.61 = (bf16[16,2176]{1,0:T(8,128)(2,1)}, bf16[16,2176]{1,0:T(8,128)(2,1)S(1)}, u32[]{:S(2)}, u32[]{:S(2)}) collective-permute-start(bf16[16,2176]{1,0:T(8,128)(2,1)} %get-tuple-element.154), channel_id=1, source_target_pairs={{0,2},{1,3},{2,4},{3,5},{4,6},{5,7},{6,0},{7,1},{8,10},{9,11},{10,... | collective-permute-start | bytes 208904 | tf_op jit(solution)/shard_map/ppermute | solution.py:322
  126.1 26.5 %collective-permute-start.62 = (bf16[16,2176]{1,0:T(8,128)(2,1)}, bf16[16,2176]{1,0:T(8,128)(2,1)S(1)}, u32[]{:S(2)}, u32[]{:S(2)}) collective-permute-start(bf16[16,2176]{1,0:T(8,128)(2,1)} %get-tuple-element.153), channel_id=1, source_target_pairs={{0,4},{1,5},{2,6},{3,7},{4,0},{5,1},{6,2},{7,3},{8,12},{9,13},{10,... | collective-permute-start | bytes 208904 | tf_op jit(solution)/shard_map/ppermute | solution.py:322
  126.1 26.5 %collective-permute-start.63 = (bf16[16,2176]{1,0:T(8,128)(2,1)S(1)}, bf16[16,2176]{1,0:T(8,128)(2,1)}, u32[]{:S(2)}, u32[]{:S(2)}) collective-permute-start(bf16[16,2176]{1,0:T(8,128)(2,1)S(1)} %get-tuple-element.152), channel_id=1, source_target_pairs={{0,6},{1,7},{2,0},{3,1},{4,2},{5,3},{6,4},{7,5},{8,14},{9,15},{10,... | collective-permute-start | bytes 208904 | tf_op jit(solution)/shard_map/ppermute | solution.py:322
  129.9 25.7 %copy-start.2 = (bf16[8,16,8,512]{3,2,1,0:T(8,128)(2,1)S(1)}, bf16[8,16,8,512]{3,2,1,0:T(8,128)(2,1)}, u32[]{:S(2)}) copy-start(bf16[8,16,8,512]{3,2,1,0:T(8,128)(2,1)} %get-tuple-element.129) | copy-start | bytes 3145732
  129.9 25.7 %copy-start.4 = (bf16[8,16,8,512]{3,2,1,0:T(8,128)(2,1)S(1)}, bf16[8,16,8,512]{3,2,1,0:T(8,128)(2,1)}, u32[]{:S(2)}) copy-start(bf16[8,16,8,512]{3,2,1,0:T(8,128)(2,1)} %get-tuple-element.139) | copy-start | bytes 3145732
  130.0 22.6 %collective-permute-start.42 = (bf16[2,3,16,8,512]{4,3,2,1,0:T(8,128)(2,1)S(1)}, bf16[2,3,16,8,512]{4,3,2,1,0:T(8,128)(2,1)}, u32[]{:S(2)}, u32[]{:S(2)}) collective-permute-start(bf16[2,3,16,8,512]{4,3,2,1,0:T(8,128)(2,1)S(1)} %param.42), channel_id=1, source_target_pairs={{0,8},{1,9},{2,10},{3,11},{4,12},{5,13},{6,14},{7,15},{8,16},{9,17... | collective-permute-start | bytes 2359304 | tf_op jit(solution)/shard_map/cond/branch_18_fun/ppermute | solution.py:279
  153.5 4.4 %collective-permute-start.65 = (bf16[16,2176]{1,0:T(8,128)(2,1)S(1)}, bf16[16,2176]{1,0:T(8,128)(2,1)S(1)}, u32[]{:S(2)}, u32[]{:S(2)}) collective-permute-start(bf16[16,2176]{1,0:T(8,128)(2,1)S(1)} %get-tuple-element.144), channel_id=1, source_target_pairs={{0,24},{8,0},{16,8},{24,16},{1,25},{9,1},{17,9},{25,17},{2,26},{10... | collective-permute-start | bytes 208904 | tf_op jit(solution)/shard_map/ppermute | solution.py:322
  153.6 4.4 %collective-permute-start.66 = (bf16[16,2176]{1,0:T(8,128)(2,1)S(1)}, bf16[16,2176]{1,0:T(8,128)(2,1)S(1)}, u32[]{:S(2)}, u32[]{:S(2)}) collective-permute-start(bf16[16,2176]{1,0:T(8,128)(2,1)S(1)} %get-tuple-element.144), channel_id=1, source_target_pairs={{0,16},{8,24},{16,0},{24,8},{1,17},{9,25},{17,1},{25,9},{2,18},{10... | collective-permute-start | bytes 208904 | tf_op jit(solution)/shard_map/ppermute | solution.py:322
  153.7 5.7 %collective-permute-start.67 = (bf16[16,2176]{1,0:T(8,128)(2,1)S(1)}, bf16[16,2176]{1,0:T(8,128)(2,1)S(1)}, u32[]{:S(2)}, u32[]{:S(2)}) collective-permute-start(bf16[16,2176]{1,0:T(8,128)(2,1)S(1)} %get-tuple-element.144), channel_id=1, source_target_pairs={{0,8},{8,16},{16,24},{24,0},{1,9},{9,17},{17,25},{25,1},{2,10},{10... | collective-permute-start | bytes 208904 | tf_op jit(solution)/shard_map/ppermute | solution.py:322
  157.5 2.0 %copy-start.3 = (bf16[8,16,8,512]{3,2,1,0:T(8,128)(2,1)}, bf16[8,16,8,512]{3,2,1,0:T(8,128)(2,1)S(1)}, u32[]{:S(2)}) copy-start(bf16[8,16,8,512]{3,2,1,0:T(8,128)(2,1)S(1)} %get-tuple-element.151) | copy-start | bytes 3145732
  157.6 2.0 %copy-start.5 = (bf16[8,16,8,512]{3,2,1,0:T(8,128)(2,1)}, bf16[8,16,8,512]{3,2,1,0:T(8,128)(2,1)S(1)}, u32[]{:S(2)}) copy-start(bf16[8,16,8,512]{3,2,1,0:T(8,128)(2,1)S(1)} %get-tuple-element.150) | copy-start | bytes 3145732
where the time goes:
time: 162 us
  waiting for transfers between devices  71.9 us (44%)
  starting transfers between devices  36 us (22%)
  Pallas kernels  32.4 us (20%)
  other arithmetic  10.5 us (6%)
  local copies, waits for them, and re-layouts  7.15 us (4%)
  between operations  3.54 us (2%)
    ppermute x6, waiting for transfers between devices, route(): lax.ppermute(array, BOTH, [(t, s) if back else (s, t) for s, t in flat])  50.2 us
    pallas_call x1, Pallas kernels, block_pass(): pl.pallas_call(block_kernel, grid_spec=pltpu.PrefetchScalarGridSpec(num_s...  32.4 us
    ppermute x16, starting transfers between devices, permuted(): return lax.ppermute(array, axis, [(n, target(n)) for n in range(count)])  25 us
    ppermute x16, waiting for transfers between devices, permuted(): return lax.ppermute(array, axis, [(n, target(n)) for n in range(count)])  21.7 us
    ppermute x6, starting transfers between devices, route(): lax.ppermute(array, BOTH, [(t, s) if back else (s, t) for s, t in flat])  11 us
  transfers between devices with their start and end apart: 22, of which 11 were waited for; matrix products, arithmetic and copies ran while one was open for 7% of the time, Pallas kernels for 0%

commit v1 on v0

--- a/solution.py
+++ b/solution.py
@@ -151,9 +151,9 @@
             now = ready
             if n + 1 < heads:
                 ready = products(n + 1)
-            before, softened = softened, forward(n, now)
-            if before is not None:
-                backward(n - 1, before)
+            if softened is not None:
+                backward(n - 1, softened)
+            softened = forward(n, now)
         backward(heads - 1, softened)
         for g in range(at_once):
             base = pl.multiple_of((step * at_once + g) * LANES, LANES)
@@ -377,10 +377,10 @@
     else:
         groups = [list(range(core, n_z * cores, cores)) for core in range(cores)]
         mine = [lax.all_gather(shard, "azi", axis=0, axis_index_groups=groups)]
+    main = radial_strip(strip, shift_rad, hops, False)
+    main, mine, side = lax.optimization_barrier((main, mine, side))
+    following = beside(main, False)
     side = beside(side, False)
-    main = radial_strip(strip, shift_rad, hops, False)
-    main, side, mine = lax.optimization_barrier((main, side, mine))
-    following = beside(main, False)
     if split:
         mine = jnp.stack(mine)
         mine = [mine, over_rad(mine, lambda n: n // 2 * 2 + (n + 1) % 2)]

time: 162 us -> 154 us (0.951)
  waiting for transfers between devices: 71.9 us -> 62.9 us
  starting transfers between devices: 36 us -> 33.1 us
    ppermute x6, waiting for transfers between devices: 50.2 us -> 38.4 us  [route(): lax.ppermute(array, BOTH, [(t, s) if back else (s, t) for s, t in flat])]
    ppermute x16, waiting for transfers between devices: 21.7 us -> 24.5 us  [permuted(): return lax.ppermute(array, axis, [(n, target(n)) for n in range(count)])]
    ppermute x6, starting transfers between devices: 11 us -> 8.69 us  [route(): lax.ppermute(array, BOTH, [(t, s) if back else (s, t) for s, t in flat])]
  transfers between devices with their start and end apart: 22 -> 22, of which waited for: 11 -> 11; matrix products, arithmetic and copies ran while one was open for 7% -> 9% of each run, Pallas kernels for 0% -> 0%
where the time goes in v1:
time: 154 us; the launch traced here: 152 us
  waiting for transfers between devices  62.9 us (41%)
  starting transfers between devices  33.1 us (21%)
  Pallas kernels  32.8 us (21%)
  other arithmetic  11.4 us (7%)
  local copies, waits for them, and re-layouts  8.51 us (6%)
  between operations  3.51 us (2%)
    ppermute x6, waiting for transfers between devices, route(): lax.ppermute(array, BOTH, [(t, s) if back else (s, t) for s, t in flat])  38.4 us
    pallas_call x1, Pallas kernels, block_pass(): pl.pallas_call(block_kernel, grid_spec=pltpu.PrefetchScalarGridSpec(num_s...  32.8 us
    ppermute x16, waiting for transfers between devices, permuted(): return lax.ppermute(array, axis, [(n, target(n)) for n in range(count)])  24.5 us
    ppermute x16, starting transfers between devices, permuted(): return lax.ppermute(array, axis, [(n, target(n)) for n in range(count)])  24.4 us
    ppermute x6, starting transfers between devices, route(): lax.ppermute(array, BOTH, [(t, s) if back else (s, t) for s, t in flat])  8.69 us
  transfers between devices with their start and end apart: 22, of which 11 were waited for; matrix products, arithmetic and copies ran while one was open for 9% of the time, Pallas kernels for 0%

profile of v1, /device:TPU:0, one launch (start us, length us, event | category | flops | bytes accessed | tf_op | source)
XLA Modules:
  0.0 152.3 jit_solution(2449630140517031305)
XLA Ops:
  0.6 0.9 fusion.11
  1.6 5.1 %collective-permute-start.48 = (bf16[32,2048]{1,0:T(8,128)(2,1)S(1)}, bf16[32,2048]{1,0:T(8,128)(2,1)S(1)}, u32[]{:S(2)}, u32[]{:S(2)}) collective-permute-start(bf16[32,2048]{1,0:T(8,128)(2,1)S(1)} %fusion.11), channel_id=1, source_target_pairs={{0,6},{1,7},{2,0},{3,1},{4,2},{5,3},{6,4},{7,5},{8,14},{9,15},{10,... | collective-permute-start | bytes 393224 | tf_op jit(solution)/shard_map/ppermute | solution.py:322
  6.7 1.0 collective-permute-start.50
  7.7 1.3 fusion.13
  10.3 1.2 slice_bitcast_fusion.2
  11.5 1.2 slice_bitcast_fusion
  13.5 18.7 %conditional.2 = (bf16[2,3,16,8,512]{4,3,2,1,0:T(8,128)(2,1)}) conditional(s32[]{:T(128)} %clamp.4, bf16[2,3,16,8,512]{4,3,2,1,0:T(8,128)(2,1)S(1)} %pad_maximum_fusion.1, bf16[2,3,16,8,512]{4,3,2,1,0:T(8,128)(2,1)S(1)} %pad_maximum_fusion.1, bf16[2,3,16,8,512]{4,3,2,1,0:T(8,128)(2,1)S(1)} %pad_maximum_fusion.1, ...), branch_computations={%region_0.1_spmd, %region_1.2_spmd, %region_2.3_spmd, %region_3.4_... | conditional | bytes 4456498 | solution.py:301
  13.5 3.6 %collective-permute-start.17 = (bf16[2,3,16,8,512]{4,3,2,1,0:T(8,128)(2,1)S(1)}, bf16[2,3,16,8,512]{4,3,2,1,0:T(8,128)(2,1)}, u32[]{:S(2)}, u32[]{:S(2)}) collective-permute-start(bf16[2,3,16,8,512]{4,3,2,1,0:T(8,128)(2,1)S(1)} %param.17), channel_id=1, source_target_pairs={{8,0},{9,1},{10,2},{11,3},{12,4},{13,5},{14,6},{15,7},{16,8},{17,9... | collective-permute-start | bytes 2359304 | tf_op jit(solution)/shard_map/cond/branch_17_fun/ppermute | solution.py:279
  17.2 15.0 %collective-permute-done.17 = bf16[2,3,16,8,512]{4,3,2,1,0:T(8,128)(2,1)} collective-permute-done((bf16[2,3,16,8,512]{4,3,2,1,0:T(8,128)(2,1)S(1)}, bf16[2,3,16,8,512]{4,3,2,1,0:T(8,128)(2,1)}, u32[]{:S(2)}, u32[]{:S(2)}) %collective-permute-start.17) | collective-permute-done | bytes 786464 | tf_op jit(solution)/shard_map/cond/branch_17_fun/ppermute | solution.py:279
  32.3 2.5 %collective-permute-start.53 = (bf16[4,32,2048]{2,1,0:T(8,128)(2,1)S(1)}, bf16[4,32,2048]{2,1,0:T(8,128)(2,1)S(1)}, u32[]{:S(2)}, u32[]{:S(2)}) collective-permute-start(bf16[4,32,2048]{2,1,0:T(8,128)(2,1)S(1)} %pad_maximum_fusion.2.refs_6_), channel_id=1, source_target_pairs={{0,8},{8,0},{16,24},{24,16},{1,9},{9,1},{17,25},{25,17},{2,10},{10... | collective-permute-start | bytes 1572872 | tf_op jit(solution)/shard_map/ppermute | solution.py:322
  34.8 1.4 collective-permute-start.51
  36.3 1.7 %collective-permute-start.52 = (bf16[2,3,16,8,512]{4,3,2,1,0:T(8,128)(2,1)}, bf16[2,3,16,8,512]{4,3,2,1,0:T(8,128)(2,1)}, u32[]{:S(2)}, u32[]{:S(2)}) collective-permute-start(bf16[2,3,16,8,512]{4,3,2,1,0:T(8,128)(2,1)} %get-tuple-element.161.refs_3_), channel_id=1, source_target_pairs={{1,0},{2,1},{3,2},{4,3},{5,4},{6,5},{7,6},{0,7},{9,8},{10,9},{11,1... | collective-permute-start | bytes 2359304 | tf_op jit(solution)/shard_map/ppermute | solution.py:279
  38.0 9.6 %collective-permute-done.53.refs_7_ = bf16[4,32,2048]{2,1,0:T(8,128)(2,1)S(1)} collective-permute-done((bf16[4,32,2048]{2,1,0:T(8,128)(2,1)S(1)}, bf16[4,32,2048]{2,1,0:T(8,128)(2,1)S(1)}, u32[]{:S(2)}, u32[]{:S(2)}) %collective-permute-start.53) | collective-permute-done | bytes 524320 | tf_op jit(solution)/shard_map/ppermute | solution.py:322
  48.4 0.7 stack.137.info_ref
  49.0 6.7 %collective-permute-done.52.refs_4_ = bf16[2,3,16,8,512]{4,3,2,1,0:T(8,128)(2,1)} collective-permute-done((bf16[2,3,16,8,512]{4,3,2,1,0:T(8,128)(2,1)}, bf16[2,3,16,8,512]{4,3,2,1,0:T(8,128)(2,1)}, u32[]{:S(2)}, u32[]{:S(2)}) %collective-permute-start.52) | collective-permute-done | bytes 786464 | tf_op jit(solution)/shard_map/ppermute | solution.py:279
  55.7 0.9 copy-done.8
  56.7 32.8 %block_pass.1 = (bf16[8,16,8,512]{3,2,1,0:T(8,128)(2,1)}, bf16[8,16,8,512]{3,2,1,0:T(8,128)(2,1)}, bf16[2,3,16,8,512]{4,3,2,1,0:T(8,128)(2,1)}, bf16[2,8,7,8,512...) custom-call(s32[6]{0:T(128)} %stack.137.info_ref, bf16[8,16,8,512]{3,2,1,0:T(8,128)(2,1)} %refs_0_.1, ...), custom_call_target="tpu_custom_call" | custom-call | flops 6442450944 | bytes 16777216 | tf_op jit(solution)/shard_map/block_pass/pallas_call | solution.py:240
  89.5 1.5 dynamic-slice_bitcast_fusion
  91.0 1.4 collective-permute-start.57
  92.5 2.8 %collective-permute-done.57 = bf16[4,4,16,2176]{3,2,1,0:T(8,128)(2,1)} collective-permute-done((bf16[4,4,16,2176]{3,2,1,0:T(8,128)(2,1)S(1)}, bf16[4,4,16,2176]{3,2,1,0:T(8,128)(2,1)}, u32[]{:S(2)}, u32[]{:S(2)}) %collective-permute-start.57) | collective-permute-done | bytes 1114144 | tf_op jit(solution)/shard_map/ppermute | solution.py:322
  95.3 1.5 fusion
  96.8 0.9 dynamic-slice_bitcast_fusion.3
  98.0 2.7 %collective-permute-start.59 = (bf16[4,16,2176]{2,1,0:T(8,128)(2,1)}, bf16[4,16,2176]{2,1,0:T(8,128)(2,1)}, u32[]{:S(2)}, u32[]{:S(2)}) collective-permute-start(bf16[4,16,2176]{2,1,0:T(8,128)(2,1)} %get-tuple-element.147), channel_id=1, source_target_pairs={{0,16},{8,24},{16,0},{24,8},{1,17},{9,25},{17,1},{25,9},{2,18},{10... | collective-permute-start | bytes 835592 | tf_op jit(solution)/shard_map/ppermute | solution.py:322
  100.6 2.9 %collective-permute-start.60 = (bf16[4,16,2176]{2,1,0:T(8,128)(2,1)S(1)}, bf16[4,16,2176]{2,1,0:T(8,128)(2,1)}, u32[]{:S(2)}, u32[]{:S(2)}) collective-permute-start(bf16[4,16,2176]{2,1,0:T(8,128)(2,1)S(1)} %get-tuple-element.146), channel_id=1, source_target_pairs={{0,24},{8,0},{16,8},{24,16},{1,25},{9,1},{17,9},{25,17},{2,26},{10... | collective-permute-start | bytes 835592 | tf_op jit(solution)/shard_map/ppermute | solution.py:322
  103.5 0.6 iota_compare_fusion.2
  104.1 0.7 iota_compare_fusion
  104.8 1.1 collective-permute-done.56
  105.9 2.5 %collective-permute-done.58 = bf16[4,16,2176]{2,1,0:T(8,128)(2,1)} collective-permute-done((bf16[4,16,2176]{2,1,0:T(8,128)(2,1)}, bf16[4,16,2176]{2,1,0:T(8,128)(2,1)}, u32[]{:S(2)}, u32[]{:S(2)}) %collective-permute-start.58) | collective-permute-done | bytes 278560 | tf_op jit(solution)/shard_map/ppermute | solution.py:322
  108.4 5.4 %collective-permute-done.59 = bf16[4,16,2176]{2,1,0:T(8,128)(2,1)} collective-permute-done((bf16[4,16,2176]{2,1,0:T(8,128)(2,1)}, bf16[4,16,2176]{2,1,0:T(8,128)(2,1)}, u32[]{:S(2)}, u32[]{:S(2)}) %collective-permute-start.59) | collective-permute-done | bytes 278560 | tf_op jit(solution)/shard_map/ppermute | solution.py:322
  113.8 1.5 collective-permute-done.60
  115.3 1.3 fusion.3
  116.5 0.7 dynamic-slice_bitcast_fusion.4
  117.2 1.9 %collective-permute-start.62 = (bf16[16,2176]{1,0:T(8,128)(2,1)}, bf16[16,2176]{1,0:T(8,128)(2,1)S(1)}, u32[]{:S(2)}, u32[]{:S(2)}) collective-permute-start(bf16[16,2176]{1,0:T(8,128)(2,1)} %get-tuple-element.153), channel_id=1, source_target_pairs={{0,4},{1,5},{2,6},{3,7},{4,0},{5,1},{6,2},{7,3},{8,12},{9,13},{10,... | collective-permute-start | bytes 208904 | tf_op jit(solution)/shard_map/ppermute | solution.py:322
  119.1 1.9 %collective-permute-start.63 = (bf16[16,2176]{1,0:T(8,128)(2,1)S(1)}, bf16[16,2176]{1,0:T(8,128)(2,1)}, u32[]{:S(2)}, u32[]{:S(2)}) collective-permute-start(bf16[16,2176]{1,0:T(8,128)(2,1)S(1)} %get-tuple-element.152), channel_id=1, source_target_pairs={{0,6},{1,7},{2,0},{3,1},{4,2},{5,3},{6,4},{7,5},{8,14},{9,15},{10,... | collective-permute-start | bytes 208904 | tf_op jit(solution)/shard_map/ppermute | solution.py:322
  121.0 1.3 broadcast_select_fusion
  122.3 17.5 %conditional.3 = (bf16[2,3,16,8,512]{4,3,2,1,0:T(8,128)(2,1)}) conditional(s32[]{:T(128)} %clamp.4, bf16[2,3,16,8,512]{4,3,2,1,0:T(8,128)(2,1)S(1)} %broadcast_select_fusion, bf16[2,3,16,8,512]{4,3,2,1,0:T(8,128)(2,1)S(1)} %broadcast_select_fusion, bf16[2,3,16,8,512]{4,3,2,1,0:T(8,128)(2,1)S(1)} %broadcast_select_fusion, ...), branch_computations={%region_24.25_spmd, %region_25.26_spmd, %region_26.27_spmd, %regio... | conditional | bytes 4456498 | solution.py:301
  122.4 1.8 %collective-permute-start.41 = (bf16[2,3,16,8,512]{4,3,2,1,0:T(8,128)(2,1)S(1)}, bf16[2,3,16,8,512]{4,3,2,1,0:T(8,128)(2,1)}, u32[]{:S(2)}, u32[]{:S(2)}) collective-permute-start(bf16[2,3,16,8,512]{4,3,2,1,0:T(8,128)(2,1)S(1)} %param.41), channel_id=1, source_target_pairs={{0,8},{1,9},{2,10},{3,11},{4,12},{5,13},{6,14},{7,15},{8,16},{9,17... | collective-permute-start | bytes 2359304 | tf_op jit(solution)/shard_map/cond/branch_17_fun/ppermute | solution.py:279
  124.2 15.6 %collective-permute-done.41 = bf16[2,3,16,8,512]{4,3,2,1,0:T(8,128)(2,1)} collective-permute-done((bf16[2,3,16,8,512]{4,3,2,1,0:T(8,128)(2,1)S(1)}, bf16[2,3,16,8,512]{4,3,2,1,0:T(8,128)(2,1)}, u32[]{:S(2)}, u32[]{:S(2)}) %collective-permute-start.41) | collective-permute-done | bytes 786464 | tf_op jit(solution)/shard_map/cond/branch_17_fun/ppermute | solution.py:279
  139.8 0.9 bitcast_dynamic-update-slice_fusion.6
  140.8 2.7 %collective-permute-start.65 = (bf16[16,2176]{1,0:T(8,128)(2,1)S(1)}, bf16[16,2176]{1,0:T(8,128)(2,1)S(1)}, u32[]{:S(2)}, u32[]{:S(2)}) collective-permute-start(bf16[16,2176]{1,0:T(8,128)(2,1)S(1)} %get-tuple-element.144), channel_id=1, source_target_pairs={{0,24},{8,0},{16,8},{24,16},{1,25},{9,1},{17,9},{25,17},{2,26},{10... | collective-permute-start | bytes 208904 | tf_op jit(solution)/shard_map/ppermute | solution.py:322
  143.4 1.4 collective-permute-start.66
  144.9 0.5 collective-permute-start.67
  145.8 1.5 fusion.6
  147.4 1.1 collective-permute-done.66
  148.5 1.6 %collective-permute-done.67 = bf16[16,2176]{1,0:T(8,128)(2,1)S(1)} collective-permute-done((bf16[16,2176]{1,0:T(8,128)(2,1)S(1)}, bf16[16,2176]{1,0:T(8,128)(2,1)S(1)}, u32[]{:S(2)}, u32[]{:S(2)}) %collective-permute-start.67) | collective-permute-done | bytes 69664 | tf_op jit(solution)/shard_map/ppermute | solution.py:322
  150.3 0.8 slice_multiply_fusion
  151.0 0.7 slice_multiply_fusion.1
  151.7 0.6 multiply_bitcast_fusion
  (51 shorter events, 1.4 us)
Async XLA Ops:
  1.6 30.7 %collective-permute-start.48 = (bf16[32,2048]{1,0:T(8,128)(2,1)S(1)}, bf16[32,2048]{1,0:T(8,128)(2,1)S(1)}, u32[]{:S(2)}, u32[]{:S(2)}) collective-permute-start(bf16[32,2048]{1,0:T(8,128)(2,1)S(1)} %fusion.11), channel_id=1, source_target_pairs={{0,6},{1,7},{2,0},{3,1},{4,2},{5,3},{6,4},{7,5},{8,14},{9,15},{10,... | collective-permute-start | bytes 393224 | tf_op jit(solution)/shard_map/ppermute | solution.py:322
  6.7 25.6 %collective-permute-start.49 = (bf16[32,2048]{1,0:T(8,128)(2,1)S(1)}, bf16[32,2048]{1,0:T(8,128)(2,1)S(1)}, u32[]{:S(2)}, u32[]{:S(2)}) collective-permute-start(bf16[32,2048]{1,0:T(8,128)(2,1)S(1)} %fusion.11), channel_id=1, source_target_pairs={{0,4},{1,5},{2,6},{3,7},{4,0},{5,1},{6,2},{7,3},{8,12},{9,13},{10,... | collective-permute-start | bytes 393224 | tf_op jit(solution)/shard_map/ppermute | solution.py:322
  6.7 25.6 %collective-permute-start.50 = (bf16[32,2048]{1,0:T(8,128)(2,1)S(1)}, bf16[32,2048]{1,0:T(8,128)(2,1)S(1)}, u32[]{:S(2)}, u32[]{:S(2)}) collective-permute-start(bf16[32,2048]{1,0:T(8,128)(2,1)S(1)} %fusion.11), channel_id=1, source_target_pairs={{0,2},{1,3},{2,4},{3,5},{4,6},{5,7},{6,0},{7,1},{8,10},{9,11},{10,... | collective-permute-start | bytes 393224 | tf_op jit(solution)/shard_map/ppermute | solution.py:322
  13.5 18.6 %collective-permute-start.17 = (bf16[2,3,16,8,512]{4,3,2,1,0:T(8,128)(2,1)S(1)}, bf16[2,3,16,8,512]{4,3,2,1,0:T(8,128)(2,1)}, u32[]{:S(2)}, u32[]{:S(2)}) collective-permute-start(bf16[2,3,16,8,512]{4,3,2,1,0:T(8,128)(2,1)S(1)} %param.17), channel_id=1, source_target_pairs={{8,0},{9,1},{10,2},{11,3},{12,4},{13,5},{14,6},{15,7},{16,8},{17,9... | collective-permute-start | bytes 2359304 | tf_op jit(solution)/shard_map/cond/branch_17_fun/ppermute | solution.py:279
  32.1 16.2 %copy-start.7 = (s32[3]{0:T(128)S(1)}, s32[3]{0:T(128)}, u32[]{:S(2)}) copy-start(s32[3]{0:T(128)} %param.61) | copy-start | bytes 40
  32.3 23.4 %copy-start.6 = (bf16[4,32,2048]{2,1,0:T(8,128)(2,1)}, bf16[4,32,2048]{2,1,0:T(8,128)(2,1)S(1)}, u32[]{:S(2)}) copy-start(bf16[4,32,2048]{2,1,0:T(8,128)(2,1)S(1)} %pad_maximum_fusion.2.refs_6_) | copy-start | bytes 1572868
  32.3 15.3 %collective-permute-start.53 = (bf16[4,32,2048]{2,1,0:T(8,128)(2,1)S(1)}, bf16[4,32,2048]{2,1,0:T(8,128)(2,1)S(1)}, u32[]{:S(2)}, u32[]{:S(2)}) collective-permute-start(bf16[4,32,2048]{2,1,0:T(8,128)(2,1)S(1)} %pad_maximum_fusion.2.refs_6_), channel_id=1, source_target_pairs={{0,8},{8,0},{16,24},{24,16},{1,9},{9,1},{17,25},{25,17},{2,10},{10... | collective-permute-start | bytes 1572872 | tf_op jit(solution)/shard_map/ppermute | solution.py:322
  34.8 20.9 %collective-permute-start.51 = (bf16[2,8,7,8,512]{4,3,2,1,0:T(8,128)(2,1)S(1)}, bf16[2,8,7,8,512]{4,3,2,1,0:T(8,128)(2,1)S(1)}, u32[]{:S(2)}, u32[]{:S(2)}) collective-permute-start(bf16[2,8,7,8,512]{4,3,2,1,0:T(8,128)(2,1)S(1)} %pad_maximum_fusion), channel_id=1, source_target_pairs={{1,0},{2,1},{3,2},{4,3},{5,4},{6,5},{7,6},{0,7},{9,8},{10,9},{11,1... | collective-permute-start | bytes 2752520 | tf_op jit(solution)/shard_map/ppermute | solution.py:279
  36.3 19.4 %collective-permute-start.52 = (bf16[2,3,16,8,512]{4,3,2,1,0:T(8,128)(2,1)}, bf16[2,3,16,8,512]{4,3,2,1,0:T(8,128)(2,1)}, u32[]{:S(2)}, u32[]{:S(2)}) collective-permute-start(bf16[2,3,16,8,512]{4,3,2,1,0:T(8,128)(2,1)} %get-tuple-element.161.refs_3_), channel_id=1, source_target_pairs={{1,0},{2,1},{3,2},{4,3},{5,4},{6,5},{7,6},{0,7},{9,8},{10,9},{11,1... | collective-permute-start | bytes 2359304 | tf_op jit(solution)/shard_map/ppermute | solution.py:279
  38.0 11.0 %collective-permute-start.54 = (bf16[4,32,2048]{2,1,0:T(8,128)(2,1)S(1)}, bf16[4,32,2048]{2,1,0:T(8,128)(2,1)}, u32[]{:S(2)}, u32[]{:S(2)}) collective-permute-start(bf16[4,32,2048]{2,1,0:T(8,128)(2,1)S(1)} %pad_maximum_fusion.2.refs_6_), channel_id=1, source_target_pairs={{0,1},{1,0},{2,3},{3,2},{4,5},{5,4},{6,7},{7,6},{8,9},{9,8},{10,11... | collective-permute-start | bytes 1572872 | tf_op jit(solution)/shard_map/ppermute | solution.py:322
  47.6 8.1 %copy-start.9 = (bf16[4,32,2048]{2,1,0:T(8,128)(2,1)}, bf16[4,32,2048]{2,1,0:T(8,128)(2,1)S(1)}, u32[]{:S(2)}) copy-start(bf16[4,32,2048]{2,1,0:T(8,128)(2,1)S(1)} %collective-permute-done.53.refs_7_) | copy-start | bytes 1572868
  47.6 8.1 %collective-permute-start.55 = (bf16[4,32,2048]{2,1,0:T(8,128)(2,1)S(1)}, bf16[4,32,2048]{2,1,0:T(8,128)(2,1)}, u32[]{:S(2)}, u32[]{:S(2)}) collective-permute-start(bf16[4,32,2048]{2,1,0:T(8,128)(2,1)S(1)} %collective-permute-done.53.refs_7_), channel_id=1, source_target_pairs={{0,1},{1,0},{2,3},{3,2},{4,5},{5,4},{6,7},{7,6},{8,9},{9,8},{10,11... | collective-permute-start | bytes 1572872 | tf_op jit(solution)/shard_map/ppermute | solution.py:322
  55.7 0.9 copy-start.8
  89.5 5.8 %copy-start = (bf16[2,4,4,16,2176]{4,3,2,1,0:T(8,128)(2,1)S(1)}, bf16[2,4,4,16,2176]{4,3,2,1,0:T(8,128)(2,1)}, u32[]{:S(2)}) copy-start(bf16[2,4,4,16,2176]{4,3,2,1,0:T(8,128)(2,1)} %get-tuple-element.133) | copy-start | bytes 6684676
  91.0 4.3 %collective-permute-start.57 = (bf16[4,4,16,2176]{3,2,1,0:T(8,128)(2,1)S(1)}, bf16[4,4,16,2176]{3,2,1,0:T(8,128)(2,1)}, u32[]{:S(2)}, u32[]{:S(2)}) collective-permute-start(bf16[4,4,16,2176]{3,2,1,0:T(8,128)(2,1)S(1)} %dynamic-slice_bitcast_fusion), channel_id=1, source_target_pairs={{0,1},{1,0},{2,3},{3,2},{4,5},{5,4},{6,7},{7,6},{8,9},{9,8},{10,11... | collective-permute-start | bytes 3342344 | tf_op jit(solution)/shard_map/ppermute | solution.py:322
  92.4 13.5 %collective-permute-start.56 = (bf16[2,3,16,8,512]{4,3,2,1,0:T(8,128)(2,1)}, bf16[2,3,16,8,512]{4,3,2,1,0:T(8,128)(2,1)}, u32[]{:S(2)}, u32[]{:S(2)}) collective-permute-start(bf16[2,3,16,8,512]{4,3,2,1,0:T(8,128)(2,1)} %get-tuple-element.130), channel_id=1, source_target_pairs={{0,1},{1,2},{2,3},{3,4},{4,5},{5,6},{6,7},{7,0},{8,9},{9,10},{10,1... | collective-permute-start | bytes 2359304 | tf_op jit(solution)/shard_map/ppermute | solution.py:279
  97.7 23.4 %copy-start.1 = (bf16[2,3,16,8,512]{4,3,2,1,0:T(8,128)(2,1)S(1)}, bf16[2,3,16,8,512]{4,3,2,1,0:T(8,128)(2,1)}, u32[]{:S(2)}) copy-start(bf16[2,3,16,8,512]{4,3,2,1,0:T(8,128)(2,1)} %get-tuple-element.130) | copy-start | bytes 2359300
  97.7 10.7 %collective-permute-start.58 = (bf16[4,16,2176]{2,1,0:T(8,128)(2,1)}, bf16[4,16,2176]{2,1,0:T(8,128)(2,1)}, u32[]{:S(2)}, u32[]{:S(2)}) collective-permute-start(bf16[4,16,2176]{2,1,0:T(8,128)(2,1)} %get-tuple-element.145), channel_id=1, source_target_pairs={{0,8},{8,16},{16,24},{24,0},{1,9},{9,17},{17,25},{25,1},{2,10},{10... | collective-permute-start | bytes 835592 | tf_op jit(solution)/shard_map/ppermute | solution.py:322
  98.0 15.8 %collective-permute-start.59 = (bf16[4,16,2176]{2,1,0:T(8,128)(2,1)}, bf16[4,16,2176]{2,1,0:T(8,128)(2,1)}, u32[]{:S(2)}, u32[]{:S(2)}) collective-permute-start(bf16[4,16,2176]{2,1,0:T(8,128)(2,1)} %get-tuple-element.147), channel_id=1, source_target_pairs={{0,16},{8,24},{16,0},{24,8},{1,17},{9,25},{17,1},{25,9},{2,18},{10... | collective-permute-start | bytes 835592 | tf_op jit(solution)/shard_map/ppermute | solution.py:322
  100.6 14.6 %collective-permute-start.60 = (bf16[4,16,2176]{2,1,0:T(8,128)(2,1)S(1)}, bf16[4,16,2176]{2,1,0:T(8,128)(2,1)}, u32[]{:S(2)}, u32[]{:S(2)}) collective-permute-start(bf16[4,16,2176]{2,1,0:T(8,128)(2,1)S(1)} %get-tuple-element.146), channel_id=1, source_target_pairs={{0,24},{8,0},{16,8},{24,16},{1,25},{9,1},{17,9},{25,17},{2,26},{10... | collective-permute-start | bytes 835592 | tf_op jit(solution)/shard_map/ppermute | solution.py:322
  105.9 33.9 %collective-permute-start.64 = (bf16[2,8,7,8,512]{4,3,2,1,0:T(8,128)(2,1)}, bf16[2,8,7,8,512]{4,3,2,1,0:T(8,128)(2,1)S(1)}, u32[]{:S(2)}, u32[]{:S(2)}) collective-permute-start(bf16[2,8,7,8,512]{4,3,2,1,0:T(8,128)(2,1)} %get-tuple-element.136), channel_id=1, source_target_pairs={{0,1},{1,2},{2,3},{3,4},{4,5},{5,6},{6,7},{7,0},{8,9},{9,10},{10,1... | collective-permute-start | bytes 2752520 | tf_op jit(solution)/shard_map/ppermute | solution.py:279
  117.2 22.6 %collective-permute-start.61 = (bf16[16,2176]{1,0:T(8,128)(2,1)}, bf16[16,2176]{1,0:T(8,128)(2,1)S(1)}, u32[]{:S(2)}, u32[]{:S(2)}) collective-permute-start(bf16[16,2176]{1,0:T(8,128)(2,1)} %get-tuple-element.154), channel_id=1, source_target_pairs={{0,2},{1,3},{2,4},{3,5},{4,6},{5,7},{6,0},{7,1},{8,10},{9,11},{10,... | collective-permute-start | bytes 208904 | tf_op jit(solution)/shard_map/ppermute | solution.py:322
  117.2 22.6 %collective-permute-start.62 = (bf16[16,2176]{1,0:T(8,128)(2,1)}, bf16[16,2176]{1,0:T(8,128)(2,1)S(1)}, u32[]{:S(2)}, u32[]{:S(2)}) collective-permute-start(bf16[16,2176]{1,0:T(8,128)(2,1)} %get-tuple-element.153), channel_id=1, source_target_pairs={{0,4},{1,5},{2,6},{3,7},{4,0},{5,1},{6,2},{7,3},{8,12},{9,13},{10,... | collective-permute-start | bytes 208904 | tf_op jit(solution)/shard_map/ppermute | solution.py:322
  119.1 20.7 %collective-permute-start.63 = (bf16[16,2176]{1,0:T(8,128)(2,1)S(1)}, bf16[16,2176]{1,0:T(8,128)(2,1)}, u32[]{:S(2)}, u32[]{:S(2)}) collective-permute-start(bf16[16,2176]{1,0:T(8,128)(2,1)S(1)} %get-tuple-element.152), channel_id=1, source_target_pairs={{0,6},{1,7},{2,0},{3,1},{4,2},{5,3},{6,4},{7,5},{8,14},{9,15},{10,... | collective-permute-start | bytes 208904 | tf_op jit(solution)/shard_map/ppermute | solution.py:322
  122.3 23.1 %copy-start.2 = (bf16[8,16,8,512]{3,2,1,0:T(8,128)(2,1)S(1)}, bf16[8,16,8,512]{3,2,1,0:T(8,128)(2,1)}, u32[]{:S(2)}) copy-start(bf16[8,16,8,512]{3,2,1,0:T(8,128)(2,1)} %get-tuple-element.129) | copy-start | bytes 3145732
  122.3 23.1 %copy-start.4 = (bf16[8,16,8,512]{3,2,1,0:T(8,128)(2,1)S(1)}, bf16[8,16,8,512]{3,2,1,0:T(8,128)(2,1)}, u32[]{:S(2)}) copy-start(bf16[8,16,8,512]{3,2,1,0:T(8,128)(2,1)} %get-tuple-element.139) | copy-start | bytes 3145732
  122.4 17.4 %collective-permute-start.41 = (bf16[2,3,16,8,512]{4,3,2,1,0:T(8,128)(2,1)S(1)}, bf16[2,3,16,8,512]{4,3,2,1,0:T(8,128)(2,1)}, u32[]{:S(2)}, u32[]{:S(2)}) collective-permute-start(bf16[2,3,16,8,512]{4,3,2,1,0:T(8,128)(2,1)S(1)} %param.41), channel_id=1, source_target_pairs={{0,8},{1,9},{2,10},{3,11},{4,12},{5,13},{6,14},{7,15},{8,16},{9,17... | collective-permute-start | bytes 2359304 | tf_op jit(solution)/shard_map/cond/branch_17_fun/ppermute | solution.py:279
  140.8 6.6 %collective-permute-start.65 = (bf16[16,2176]{1,0:T(8,128)(2,1)S(1)}, bf16[16,2176]{1,0:T(8,128)(2,1)S(1)}, u32[]{:S(2)}, u32[]{:S(2)}) collective-permute-start(bf16[16,2176]{1,0:T(8,128)(2,1)S(1)} %get-tuple-element.144), channel_id=1, source_target_pairs={{0,24},{8,0},{16,8},{24,16},{1,25},{9,1},{17,9},{25,17},{2,26},{10... | collective-permute-start | bytes 208904 | tf_op jit(solution)/shard_map/ppermute | solution.py:322
  143.4 5.1 %collective-permute-start.66 = (bf16[16,2176]{1,0:T(8,128)(2,1)S(1)}, bf16[16,2176]{1,0:T(8,128)(2,1)S(1)}, u32[]{:S(2)}, u32[]{:S(2)}) collective-permute-start(bf16[16,2176]{1,0:T(8,128)(2,1)S(1)} %get-tuple-element.144), channel_id=1, source_target_pairs={{0,16},{8,24},{16,0},{24,8},{1,17},{9,25},{17,1},{25,9},{2,18},{10... | collective-permute-start | bytes 208904 | tf_op jit(solution)/shard_map/ppermute | solution.py:322
  144.9 5.2 %collective-permute-start.67 = (bf16[16,2176]{1,0:T(8,128)(2,1)S(1)}, bf16[16,2176]{1,0:T(8,128)(2,1)S(1)}, u32[]{:S(2)}, u32[]{:S(2)}) collective-permute-start(bf16[16,2176]{1,0:T(8,128)(2,1)S(1)} %get-tuple-element.144), channel_id=1, source_target_pairs={{0,8},{8,16},{16,24},{24,0},{1,9},{9,17},{17,25},{25,1},{2,10},{10... | collective-permute-start | bytes 208904 | tf_op jit(solution)/shard_map/ppermute | solution.py:322
  147.3 2.9 %copy-start.3 = (bf16[8,16,8,512]{3,2,1,0:T(8,128)(2,1)}, bf16[8,16,8,512]{3,2,1,0:T(8,128)(2,1)S(1)}, u32[]{:S(2)}) copy-start(bf16[8,16,8,512]{3,2,1,0:T(8,128)(2,1)S(1)} %get-tuple-element.151) | copy-start | bytes 3145732
  147.3 2.9 %copy-start.5 = (bf16[8,16,8,512]{3,2,1,0:T(8,128)(2,1)}, bf16[8,16,8,512]{3,2,1,0:T(8,128)(2,1)S(1)}, u32[]{:S(2)}) copy-start(bf16[8,16,8,512]{3,2,1,0:T(8,128)(2,1)S(1)} %get-tuple-element.150) | copy-start | bytes 3145732

commit v2 on v0

--- a/solution.py
+++ b/solution.py
@@ -1,3 +1,5 @@
+import functools
+
 import jax
 import jax.numpy as jnp
 from jax import lax
@@ -24,10 +26,10 @@
 
 def block_kernel(info_ref, *refs):
     x_ref, g_ref, side_ref, main_ref, next_ref, gain_ref = refs[:6]
-    weight_refs, refs = refs[6:-20], refs[-20:]
-    y_ref, dx_ref, strip_ref, rim_ref, gw_ref, gg_ref, f_s, w_ref = refs[:8]
-    x_s, g_s, xhat_s, qkv_s, da_s, att_s, dqkv_s = refs[8:15]
-    hid_all, att_all, gs_all, dqkv_all, gain_s = refs[15:20]
+    weight_refs, refs = refs[6:-21], refs[-21:]
+    y_ref, dx_ref, strip_ref, rim_ref, gw_ref, given_ref, gg_ref, f_s, w_ref = refs[:9]
+    x_s, g_s, xhat_s, qkv_s, da_s, att_s, dqkv_s = refs[9:16]
+    hid_all, att_all, gs_all, dqkv_all, gain_s = refs[16:21]
     step = pl.program_id(0)
     steps = pl.num_programs(0)
     rows, cols, depth, width = x_ref.shape
@@ -207,18 +209,26 @@
             gw_ref[:, : 3 * width] = g_qkv
             gw_ref[:, 3 * width:] = g_out
         else:
-            cores, n_rad, n_z, part, _ = gw_ref.shape
+            n_rad, n_z, part, _ = gw_ref.shape
             extra = jnp.concatenate(
                 [gain_s[:, n * LANES:(n + 1) * LANES] for n in range(width // LANES)]
                 + [jnp.zeros((part - width // LANES, LANES), jnp.float32)],
                 axis=0,
             ).astype(jnp.bfloat16)
-            for n in range(cores * n_rad * n_z):
-                z, core, i = n // n_rad // cores, n // n_rad % cores, n % n_rad
-                here = gw_ref.at[core, i, z]
-                here[:, : 3 * width] = g_qkv[n * part:(n + 1) * part]
-                here[:, 3 * width: 4 * width] = g_out[n * part:(n + 1) * part]
-                here[:, 4 * width:] = extra
+
+            def place(kept_core):
+                for n in range(2 * n_rad * n_z):
+                    z, core, i = n // n_rad // 2, n // n_rad % 2, n % n_rad
+                    rad_ahead = lax.rem(i + n_rad - info_ref[6], n_rad)
+                    z_ahead = lax.rem(z + n_z - info_ref[7], n_z)
+                    ref = gw_ref if core == kept_core else given_ref
+                    here = ref.at[rad_ahead, z_ahead]
+                    here[:, : 3 * width] = g_qkv[n * part:(n + 1) * part]
+                    here[:, 3 * width: 4 * width] = g_out[n * part:(n + 1) * part]
+                    here[:, 4 * width:] = extra
+
+            for kept_core in range(2):
+                pl.when(info_ref[4] == kept_core)(functools.partial(place, kept_core))
 
 
 def block_pass(info, x, g, side, main, following, gain, weights, term_shape):
@@ -235,7 +245,7 @@
     ins = (x, g, side, main, following, gain) + tuple(weights)
     outs = [
         (x.shape, bf), (x.shape, bf), (strip_shape, bf), (rim_shape, bf),
-        (term_shape, bf), ((1, width), f32),
+        (term_shape, bf), (term_shape, bf), ((1, width), f32),
     ]
     return pl.pallas_call(
         block_kernel,
@@ -322,27 +332,10 @@
     return lax.ppermute(array, axis, [(n, target(n)) for n in range(count)])
 
 
-def scatter_sum(pieces, index, send, hold=lambda arrays: arrays):
+def scatter_sum(pieces, send, hold=lambda arrays: arrays):
     count = pieces.shape[0]
-    if count > 4 and count % 2 == 0:
-        half = count // 2
-        halves = pieces.reshape((2, half) + pieces.shape[1:])
-        upper = index // half
-        kept = lax.dynamic_index_in_dim(halves, upper, 0, keepdims=False)
-        given = lax.dynamic_index_in_dim(halves, 1 - upper, 0, keepdims=False)
-        got = send(given, lambda n: (n + half) % count)
-        kept = (kept.astype(jnp.float32) + got.astype(jnp.float32)).astype(pieces.dtype)
-        return scatter_sum(
-            kept,
-            index % half,
-            lambda array, to: send(array, lambda n: n // half * half + to(n % half)),
-            hold,
-        )
-    total = lax.dynamic_index_in_dim(pieces, index, 0, keepdims=False).astype(jnp.float32)
-    arrived = []
-    for d in range(1, count):
-        given = lax.dynamic_index_in_dim(pieces, (index + d) % count, 0, keepdims=False)
-        arrived.append(send(given, lambda n: (n + d) % count))
+    arrived = [send(pieces[d], lambda n: (n + d) % count) for d in range(1, count)]
+    total = pieces[0].astype(jnp.float32)
     for got in hold(arrived):
         total = total + got.astype(jnp.float32)
     return total.astype(pieces.dtype)
@@ -414,11 +407,12 @@
     wrap_col = jnp.where(last, amount % cols_dev, shift_azi)
     at_core = lax.axis_index("azi") % cores
     info = [shift_rad, shift_azi, wrap_col, first_z, at_core, first_part]
+    info += [at_rad, lax.axis_index("azi") // cores]
     info = jnp.stack([jnp.asarray(value, jnp.int32) for value in info])
     part_rows = width // n_azi // n_rad
     placed = part_rows % 16 == 0
-    pieces_shape = (cores, n_rad, n_azi // cores, part_rows, 4 * width + LANES)
-    y, dx, strip, side, term, gain = block_pass(
+    pieces_shape = (n_rad, n_azi // cores, part_rows, 4 * width + LANES)
+    y, dx, strip, side, term, given, gain = block_pass(
         info, tokens, cotangent, side, main, following, ln_gain.reshape(1, width), weights,
         pieces_shape if placed else (width, 4 * width),
     )
@@ -427,8 +421,8 @@
     side = beside(side, True)
     col = jnp.arange(cols_dev, dtype=jnp.int32).reshape(1, 1, cols_dev, 1, 1)
     if placed:
-        at_azi = lax.axis_index("azi")
-        term = scatter_sum(term, at_azi % cores, over_core(cores))
+        got = over_core(cores)(given, lambda n: (n + 1) % cores)
+        term = (term.astype(jnp.float32) + got.astype(jnp.float32)).astype(term.dtype)
         strip_back = []
 
         def beside_strip(arrays):
@@ -438,10 +432,10 @@
             strip_back.extend((back, beside_it))
             return arrays
 
-        term = scatter_sum(term, at_rad, over_rad)
+        term = scatter_sum(term, over_rad)
         following, term = lax.optimization_barrier((following, term))
         strip = jnp.where(col < wrap_col, following, strip)
-        mine = scatter_sum(term, at_azi // cores, over_z(cores), beside_strip)
+        mine = scatter_sum(term, over_z(cores), beside_strip)
         strip, side = strip_back
     else:
         strip = jnp.where(col < wrap_col, following, strip)

time: 162 us -> 178 us (1.099)
  starting transfers between devices: 36 us -> 44.2 us
  waiting for transfers between devices: 71.9 us -> 79.1 us
  other arithmetic: 10.5 us -> 8.44 us
    ppermute x16, waiting for transfers between devices: 21.7 us -> 31.2 us  [permuted(): return lax.ppermute(array, axis, [(n, target(n)) for n in range(count)])]
    ppermute x16, starting transfers between devices: 25 us -> 33.2 us  [permuted(): return lax.ppermute(array, axis, [(n, target(n)) for n in range(count)])]
    ppermute x6, waiting for transfers between devices: 50.2 us -> 47.9 us  [route(): lax.ppermute(array, BOTH, [(t, s) if back else (s, t) for s, t in flat])]
    pad x0 -> x2, local copies, waits for them, and re-layouts: none -> 1.87 us  [full_rows(): return jnp.pad(array, ((0, 0), (0, missing), (0, 0), (0, 0), (0, 0)))]
  transfers between devices with their start and end apart: 22 -> 22, of which waited for: 11 -> 10; matrix products, arithmetic and copies ran while one was open for 7% -> 7% of each run, Pallas kernels for 0% -> 0%
where the time goes in v2:
time: 178 us; the launch traced here: 176 us
  waiting for transfers between devices  79.1 us (44%)
  starting transfers between devices  44.2 us (25%)
  Pallas kernels  32.5 us (18%)
  local copies, waits for them, and re-layouts  8.46 us (5%)
  other arithmetic  8.44 us (5%)
  between operations  3.39 us (2%)
    ppermute x6, waiting for transfers between devices, route(): lax.ppermute(array, BOTH, [(t, s) if back else (s, t) for s, t in flat])  47.9 us
    ppermute x16, starting transfers between devices, permuted(): return lax.ppermute(array, axis, [(n, target(n)) for n in range(count)])  33.2 us
    pallas_call x1, Pallas kernels, block_pass(): pl.pallas_call(block_kernel, grid_spec=pltpu.PrefetchScalarGridSpec(num_s...  32.5 us
    ppermute x16, waiting for transfers between devices, permuted(): return lax.ppermute(array, axis, [(n, target(n)) for n in range(count)])  31.2 us
    ppermute x6, starting transfers between devices, route(): lax.ppermute(array, BOTH, [(t, s) if back else (s, t) for s, t in flat])  11 us
  transfers between devices with their start and end apart: 22, of which 10 were waited for; matrix products, arithmetic and copies ran while one was open for 7% of the time, Pallas kernels for 0%

profile of v2, /device:TPU:0, one launch (start us, length us, event | category | flops | bytes accessed | tf_op | source)
XLA Modules:
  0.0 176.2 jit_solution(3703492442257056704)
XLA Ops:
  0.6 1.2 slice_bitcast_fusion
  2.0 4.5 %collective-permute-start.48 = (bf16[2,8,7,8,512]{4,3,2,1,0:T(8,128)(2,1)S(1)}, bf16[2,8,7,8,512]{4,3,2,1,0:T(8,128)(2,1)S(1)}, u32[]{:S(2)}, u32[]{:S(2)}) collective-permute-start(bf16[2,8,7,8,512]{4,3,2,1,0:T(8,128)(2,1)S(1)} %pad_maximum_fusion), channel_id=1, source_target_pairs={{1,0},{2,1},{3,2},{4,3},{5,4},{6,5},{7,6},{0,7},{9,8},{10,9},{11,1... | collective-permute-start | bytes 2752520 | tf_op jit(solution)/shard_map/ppermute | solution.py:289
  6.6 1.9 %collective-permute-start.50 = (bf16[32,2048]{1,0:T(8,128)(2,1)S(1)}, bf16[32,2048]{1,0:T(8,128)(2,1)S(1)}, u32[]{:S(2)}, u32[]{:S(2)}) collective-permute-start(bf16[32,2048]{1,0:T(8,128)(2,1)S(1)} %fusion.10), channel_id=1, source_target_pairs={{0,4},{1,5},{2,6},{3,7},{4,0},{5,1},{6,2},{7,3},{8,12},{9,13},{10,... | collective-permute-start | bytes 393224 | tf_op jit(solution)/shard_map/ppermute | solution.py:332
  8.5 2.0 %collective-permute-start.49 = (bf16[32,2048]{1,0:T(8,128)(2,1)S(1)}, bf16[32,2048]{1,0:T(8,128)(2,1)S(1)}, u32[]{:S(2)}, u32[]{:S(2)}) collective-permute-start(bf16[32,2048]{1,0:T(8,128)(2,1)S(1)} %fusion.10), channel_id=1, source_target_pairs={{0,6},{1,7},{2,0},{3,1},{4,2},{5,3},{6,4},{7,5},{8,14},{9,15},{10,... | collective-permute-start | bytes 393224 | tf_op jit(solution)/shard_map/ppermute | solution.py:332
  11.1 0.6 fusion.12
  12.9 1.2 slice_bitcast_fusion.2
  14.2 22.6 %conditional.2 = (bf16[2,3,16,8,512]{4,3,2,1,0:T(8,128)(2,1)}) conditional(s32[]{:T(128)} %clamp.4, bf16[2,3,16,8,512]{4,3,2,1,0:T(8,128)(2,1)S(1)} %pad_maximum_fusion.1, bf16[2,3,16,8,512]{4,3,2,1,0:T(8,128)(2,1)S(1)} %pad_maximum_fusion.1, bf16[2,3,16,8,512]{4,3,2,1,0:T(8,128)(2,1)S(1)} %pad_maximum_fusion.1, ...), branch_computations={%region_0.1_spmd, %region_1.2_spmd, %region_2.3_spmd, %region_3.4_... | conditional | bytes 4456498 | solution.py:311
  14.2 4.0 %collective-permute-start.12 = (bf16[2,2,16,8,512]{4,3,2,1,0:T(8,128)(2,1)S(1)}, bf16[2,2,16,8,512]{4,3,2,1,0:T(8,128)(2,1)S(1)}, u32[]{:S(2)}, u32[]{:S(2)}) collective-permute-start(bf16[2,2,16,8,512]{4,3,2,1,0:T(8,128)(2,1)S(1)} %slice.133), channel_id=1, source_target_pairs={{8,0},{9,1},{10,2},{11,3},{12,4},{13,5},{14,6},{15,7},{16,8},{17,9... | collective-permute-start | bytes 1572872 | tf_op jit(solution)/shard_map/cond/branch_12_fun/ppermute | solution.py:289
  18.2 17.6 %collective-permute-done.12 = bf16[2,2,16,8,512]{4,3,2,1,0:T(8,128)(2,1)S(1)} collective-permute-done((bf16[2,2,16,8,512]{4,3,2,1,0:T(8,128)(2,1)S(1)}, bf16[2,2,16,8,512]{4,3,2,1,0:T(8,128)(2,1)S(1)}, u32[]{:S(2)}, u32[]{:S(2)}) %collective-permute-start.12) | collective-permute-done | bytes 524320 | tf_op jit(solution)/shard_map/cond/branch_12_fun/ppermute | solution.py:289
  35.8 0.9 pad.78
  36.7 7.4 %collective-permute-done.50 = bf16[32,2048]{1,0:T(8,128)(2,1)S(1)} collective-permute-done((bf16[32,2048]{1,0:T(8,128)(2,1)S(1)}, bf16[32,2048]{1,0:T(8,128)(2,1)S(1)}, u32[]{:S(2)}, u32[]{:S(2)}) %collective-permute-start.50) | collective-permute-done | bytes 131104 | tf_op jit(solution)/shard_map/ppermute | solution.py:332
  44.3 0.2 collective-permute-start.52
  44.6 0.5 collective-permute-start.54
  45.1 10.7 %collective-permute-done.53.refs_7_ = bf16[4,32,2048]{2,1,0:T(8,128)(2,1)S(1)} collective-permute-done((bf16[4,32,2048]{2,1,0:T(8,128)(2,1)S(1)}, bf16[4,32,2048]{2,1,0:T(8,128)(2,1)S(1)}, u32[]{:S(2)}, u32[]{:S(2)}) %collective-permute-start.53) | collective-permute-done | bytes 524320 | tf_op jit(solution)/shard_map/ppermute | solution.py:332
  56.3 0.6 stack.142.info_ref
  57.0 0.9 collective-permute-done.55.refs_9_
  57.8 0.2 copy-done.12
  58.0 32.5 %block_pass.1 = (bf16[8,16,8,512]{3,2,1,0:T(8,128)(2,1)}, bf16[8,16,8,512]{3,2,1,0:T(8,128)(2,1)}, bf16[2,3,16,8,512]{4,3,2,1,0:T(8,128)(2,1)}, bf16[2,8,7,8,512...) custom-call(s32[8]{0:T(128)} %stack.142.info_ref, ...), custom_call_target="tpu_custom_call" | custom-call | flops 6442450944 | bytes 16777216 | tf_op jit(solution)/shard_map/block_pass/pallas_call | solution.py:250
  90.5 13.6 %collective-permute-start.57 = (bf16[4,4,16,2176]{3,2,1,0:T(8,128)(2,1)}, bf16[4,4,16,2176]{3,2,1,0:T(8,128)(2,1)S(1)}, u32[]{:S(2)}, u32[]{:S(2)}) collective-permute-start(bf16[4,4,16,2176]{3,2,1,0:T(8,128)(2,1)} %get-tuple-element.135), channel_id=1, source_target_pairs={{0,1},{1,0},{2,3},{3,2},{4,5},{5,4},{6,7},{7,6},{8,9},{9,8},{10,11... | collective-permute-start | bytes 3342344 | tf_op jit(solution)/shard_map/ppermute | solution.py:332
  104.2 2.5 %collective-permute-done.57 = bf16[4,4,16,2176]{3,2,1,0:T(8,128)(2,1)S(1)} collective-permute-done((bf16[4,4,16,2176]{3,2,1,0:T(8,128)(2,1)}, bf16[4,4,16,2176]{3,2,1,0:T(8,128)(2,1)S(1)}, u32[]{:S(2)}, u32[]{:S(2)}) %collective-permute-start.57) | collective-permute-done | bytes 1114144 | tf_op jit(solution)/shard_map/ppermute | solution.py:332
  106.7 1.5 add_convert_fusion
  108.3 0.9 slice_bitcast_fusion.6
  109.1 1.8 %collective-permute-start.58 = (bf16[4,16,2176]{2,1,0:T(8,128)(2,1)}, bf16[4,16,2176]{2,1,0:T(8,128)(2,1)}, u32[]{:S(2)}, u32[]{:S(2)}) collective-permute-start(bf16[4,16,2176]{2,1,0:T(8,128)(2,1)} %get-tuple-element.147), channel_id=1, source_target_pairs={{0,8},{8,16},{16,24},{24,0},{1,9},{9,17},{17,25},{25,1},{2,10},{10... | collective-permute-start | bytes 835592 | tf_op jit(solution)/shard_map/ppermute | solution.py:332
  110.9 2.2 %collective-permute-start.60 = (bf16[4,16,2176]{2,1,0:T(8,128)(2,1)}, bf16[4,16,2176]{2,1,0:T(8,128)(2,1)}, u32[]{:S(2)}, u32[]{:S(2)}) collective-permute-start(bf16[4,16,2176]{2,1,0:T(8,128)(2,1)} %get-tuple-element.148), channel_id=1, source_target_pairs={{0,24},{8,0},{16,8},{24,16},{1,25},{9,1},{17,9},{25,17},{2,26},{10... | collective-permute-start | bytes 835592 | tf_op jit(solution)/shard_map/ppermute | solution.py:332
  113.1 2.9 %collective-permute-start.59 = (bf16[4,16,2176]{2,1,0:T(8,128)(2,1)S(1)}, bf16[4,16,2176]{2,1,0:T(8,128)(2,1)}, u32[]{:S(2)}, u32[]{:S(2)}) collective-permute-start(bf16[4,16,2176]{2,1,0:T(8,128)(2,1)S(1)} %get-tuple-element.149), channel_id=1, source_target_pairs={{0,16},{8,24},{16,0},{24,8},{1,17},{9,25},{17,1},{25,9},{2,18},{10... | collective-permute-start | bytes 835592 | tf_op jit(solution)/shard_map/ppermute | solution.py:332
  116.0 0.6 iota_compare_fusion
  116.7 0.6 iota_compare_fusion.2
  117.3 0.3 collective-permute-done.56
  117.6 0.9 copy-done.1
  118.4 0.4 collective-permute-start.64
  118.8 2.2 %collective-permute-done.58 = bf16[4,16,2176]{2,1,0:T(8,128)(2,1)} collective-permute-done((bf16[4,16,2176]{2,1,0:T(8,128)(2,1)}, bf16[4,16,2176]{2,1,0:T(8,128)(2,1)}, u32[]{:S(2)}, u32[]{:S(2)}) %collective-permute-start.58) | collective-permute-done | bytes 278560 | tf_op jit(solution)/shard_map/ppermute | solution.py:332
  121.0 6.6 %collective-permute-done.60 = bf16[4,16,2176]{2,1,0:T(8,128)(2,1)} collective-permute-done((bf16[4,16,2176]{2,1,0:T(8,128)(2,1)}, bf16[4,16,2176]{2,1,0:T(8,128)(2,1)}, u32[]{:S(2)}, u32[]{:S(2)}) %collective-permute-start.60) | collective-permute-done | bytes 278560 | tf_op jit(solution)/shard_map/ppermute | solution.py:332
  127.6 1.3 fusion.2
  128.9 0.7 slice_bitcast_fusion.8
  129.5 4.7 %collective-permute-start.63 = (bf16[16,2176]{1,0:T(8,128)(2,1)}, bf16[16,2176]{1,0:T(8,128)(2,1)S(1)}, u32[]{:S(2)}, u32[]{:S(2)}) collective-permute-start(bf16[16,2176]{1,0:T(8,128)(2,1)} %get-tuple-element.154), channel_id=1, source_target_pairs={{0,6},{1,7},{2,0},{3,1},{4,2},{5,3},{6,4},{7,5},{8,14},{9,15},{10,... | collective-permute-start | bytes 208904 | tf_op jit(solution)/shard_map/ppermute | solution.py:332
  134.2 0.6 collective-permute-start.61
  134.8 0.2 broadcast_select_fusion
  135.0 32.9 %conditional.3 = (bf16[2,3,16,8,512]{4,3,2,1,0:T(8,128)(2,1)}) conditional(s32[]{:T(128)} %clamp.4, bf16[2,3,16,8,512]{4,3,2,1,0:T(8,128)(2,1)S(1)} %broadcast_select_fusion, bf16[2,3,16,8,512]{4,3,2,1,0:T(8,128)(2,1)S(1)} %broadcast_select_fusion, bf16[2,3,16,8,512]{4,3,2,1,0:T(8,128)(2,1)S(1)} %broadcast_select_fusion, ...), branch_computations={%region_24.25_spmd, %region_25.26_spmd, %region_26.27_spmd, %regio... | conditional | bytes 4456498 | solution.py:311
  135.1 1.8 %collective-permute-start.36 = (bf16[2,2,16,8,512]{4,3,2,1,0:T(8,128)(2,1)S(1)}, bf16[2,2,16,8,512]{4,3,2,1,0:T(8,128)(2,1)S(1)}, u32[]{:S(2)}, u32[]{:S(2)}) collective-permute-start(bf16[2,2,16,8,512]{4,3,2,1,0:T(8,128)(2,1)S(1)} %slice.149), channel_id=1, source_target_pairs={{0,8},{1,9},{2,10},{3,11},{4,12},{5,13},{6,14},{7,15},{8,16},{9,17... | collective-permute-start | bytes 1572872 | tf_op jit(solution)/shard_map/cond/branch_12_fun/ppermute | solution.py:289
  136.9 30.0 %collective-permute-done.36 = bf16[2,2,16,8,512]{4,3,2,1,0:T(8,128)(2,1)S(1)} collective-permute-done((bf16[2,2,16,8,512]{4,3,2,1,0:T(8,128)(2,1)S(1)}, bf16[2,2,16,8,512]{4,3,2,1,0:T(8,128)(2,1)S(1)}, u32[]{:S(2)}, u32[]{:S(2)}) %collective-permute-start.36) | collective-permute-done | bytes 524320 | tf_op jit(solution)/shard_map/cond/branch_12_fun/ppermute | solution.py:289
  166.9 0.9 pad.94
  168.1 2.8 %collective-permute-start.65 = (bf16[16,2176]{1,0:T(8,128)(2,1)S(1)}, bf16[16,2176]{1,0:T(8,128)(2,1)S(1)}, u32[]{:S(2)}, u32[]{:S(2)}) collective-permute-start(bf16[16,2176]{1,0:T(8,128)(2,1)S(1)} %get-tuple-element.146), channel_id=1, source_target_pairs={{0,24},{8,0},{16,8},{24,16},{1,25},{9,1},{17,9},{25,17},{2,26},{10... | collective-permute-start | bytes 208904 | tf_op jit(solution)/shard_map/ppermute | solution.py:332
  170.9 0.4 fusion.3
  171.4 1.5 fusion.5
  172.9 0.9 collective-permute-done.65
  174.2 0.7 slice_multiply_fusion.1
  174.8 0.8 slice_multiply_fusion
  175.6 0.6 multiply_bitcast_fusion
  (64 shorter events, 1.1 us)
Async XLA Ops:
  1.9 4.7 %copy-start.8 = (bf16[64,1536]{1,0:T(8,128)(2,1)S(1)}, bf16[64,1536]{1,0:T(8,128)(2,1)}, u32[]{:S(2)}) copy-start(bf16[64,1536]{1,0:T(8,128)(2,1)} %param.58) | copy-start | bytes 589828
  1.9 4.7 %copy-start.9 = (bf16[64,512]{1,0:T(8,128)(2,1)S(1)}, bf16[64,512]{1,0:T(8,128)(2,1)}, u32[]{:S(2)}) copy-start(bf16[64,512]{1,0:T(8,128)(2,1)} %param.59) | copy-start | bytes 196612
  1.9 9.2 %copy-start.10 = (s32[3]{0:T(128)S(1)}, s32[3]{0:T(128)}, u32[]{:S(2)}) copy-start(s32[3]{0:T(128)} %param.61) | copy-start | bytes 40
  2.0 42.2 %collective-permute-start.48 = (bf16[2,8,7,8,512]{4,3,2,1,0:T(8,128)(2,1)S(1)}, bf16[2,8,7,8,512]{4,3,2,1,0:T(8,128)(2,1)S(1)}, u32[]{:S(2)}, u32[]{:S(2)}) collective-permute-start(bf16[2,8,7,8,512]{4,3,2,1,0:T(8,128)(2,1)S(1)} %pad_maximum_fusion), channel_id=1, source_target_pairs={{1,0},{2,1},{3,2},{4,3},{5,4},{6,5},{7,6},{0,7},{9,8},{10,9},{11,1... | collective-permute-start | bytes 2752520 | tf_op jit(solution)/shard_map/ppermute | solution.py:289
  6.6 30.2 %collective-permute-start.51 = (bf16[32,2048]{1,0:T(8,128)(2,1)S(1)}, bf16[32,2048]{1,0:T(8,128)(2,1)S(1)}, u32[]{:S(2)}, u32[]{:S(2)}) collective-permute-start(bf16[32,2048]{1,0:T(8,128)(2,1)S(1)} %fusion.10), channel_id=1, source_target_pairs={{0,2},{1,3},{2,4},{3,5},{4,6},{5,7},{6,0},{7,1},{8,10},{9,11},{10,... | collective-permute-start | bytes 393224 | tf_op jit(solution)/shard_map/ppermute | solution.py:332
  6.6 37.5 %collective-permute-start.50 = (bf16[32,2048]{1,0:T(8,128)(2,1)S(1)}, bf16[32,2048]{1,0:T(8,128)(2,1)S(1)}, u32[]{:S(2)}, u32[]{:S(2)}) collective-permute-start(bf16[32,2048]{1,0:T(8,128)(2,1)S(1)} %fusion.10), channel_id=1, source_target_pairs={{0,4},{1,5},{2,6},{3,7},{4,0},{5,1},{6,2},{7,3},{8,12},{9,13},{10,... | collective-permute-start | bytes 393224 | tf_op jit(solution)/shard_map/ppermute | solution.py:332
  8.5 35.7 %collective-permute-start.49 = (bf16[32,2048]{1,0:T(8,128)(2,1)S(1)}, bf16[32,2048]{1,0:T(8,128)(2,1)S(1)}, u32[]{:S(2)}, u32[]{:S(2)}) collective-permute-start(bf16[32,2048]{1,0:T(8,128)(2,1)S(1)} %fusion.10), channel_id=1, source_target_pairs={{0,6},{1,7},{2,0},{3,1},{4,2},{5,3},{6,4},{7,5},{8,14},{9,15},{10,... | collective-permute-start | bytes 393224 | tf_op jit(solution)/shard_map/ppermute | solution.py:332
  14.2 21.6 %collective-permute-start.12 = (bf16[2,2,16,8,512]{4,3,2,1,0:T(8,128)(2,1)S(1)}, bf16[2,2,16,8,512]{4,3,2,1,0:T(8,128)(2,1)S(1)}, u32[]{:S(2)}, u32[]{:S(2)}) collective-permute-start(bf16[2,2,16,8,512]{4,3,2,1,0:T(8,128)(2,1)S(1)} %slice.133), channel_id=1, source_target_pairs={{8,0},{9,1},{10,2},{11,3},{12,4},{13,5},{14,6},{15,7},{16,8},{17,9... | collective-permute-start | bytes 1572872 | tf_op jit(solution)/shard_map/cond/branch_12_fun/ppermute | solution.py:289
  44.1 13.7 %copy-start.11 = (bf16[2,8,7,8,512]{4,3,2,1,0:T(8,128)(2,1)}, bf16[2,8,7,8,512]{4,3,2,1,0:T(8,128)(2,1)S(1)}, u32[]{:S(2)}) copy-start(bf16[2,8,7,8,512]{4,3,2,1,0:T(8,128)(2,1)S(1)} %collective-permute-done.48.refs_2_) | copy-start | bytes 2752516
  44.2 13.6 %copy-start.7 = (bf16[4,32,2048]{2,1,0:T(8,128)(2,1)}, bf16[4,32,2048]{2,1,0:T(8,128)(2,1)S(1)}, u32[]{:S(2)}) copy-start(bf16[4,32,2048]{2,1,0:T(8,128)(2,1)S(1)} %pad_maximum_fusion.2.refs_6_) | copy-start | bytes 1572868
  44.2 11.5 %collective-permute-start.53 = (bf16[4,32,2048]{2,1,0:T(8,128)(2,1)S(1)}, bf16[4,32,2048]{2,1,0:T(8,128)(2,1)S(1)}, u32[]{:S(2)}, u32[]{:S(2)}) collective-permute-start(bf16[4,32,2048]{2,1,0:T(8,128)(2,1)S(1)} %pad_maximum_fusion.2.refs_6_), channel_id=1, source_target_pairs={{0,8},{8,0},{16,24},{24,16},{1,9},{9,1},{17,25},{25,17},{2,10},{10... | collective-permute-start | bytes 1572872 | tf_op jit(solution)/shard_map/ppermute | solution.py:332
  44.3 12.6 %collective-permute-start.52 = (bf16[2,3,16,8,512]{4,3,2,1,0:T(8,128)(2,1)}, bf16[2,3,16,8,512]{4,3,2,1,0:T(8,128)(2,1)S(1)}, u32[]{:S(2)}, u32[]{:S(2)}) collective-permute-start(bf16[2,3,16,8,512]{4,3,2,1,0:T(8,128)(2,1)} %get-tuple-element.163.refs_3_), channel_id=1, source_target_pairs={{1,0},{2,1},{3,2},{4,3},{5,4},{6,5},{7,6},{0,7},{9,8},{10,9},{11,1... | collective-permute-start | bytes 2359304 | tf_op jit(solution)/shard_map/ppermute | solution.py:289
  44.6 12.4 %collective-permute-start.54 = (bf16[4,32,2048]{2,1,0:T(8,128)(2,1)S(1)}, bf16[4,32,2048]{2,1,0:T(8,128)(2,1)S(1)}, u32[]{:S(2)}, u32[]{:S(2)}) collective-permute-start(bf16[4,32,2048]{2,1,0:T(8,128)(2,1)S(1)} %pad_maximum_fusion.2.refs_6_), channel_id=1, source_target_pairs={{0,1},{1,0},{2,3},{3,2},{4,5},{5,4},{6,7},{7,6},{8,9},{9,8},{10,11... | collective-permute-start | bytes 1572872 | tf_op jit(solution)/shard_map/ppermute | solution.py:332
  55.8 2.1 %copy-start.13 = (bf16[4,32,2048]{2,1,0:T(8,128)(2,1)}, bf16[4,32,2048]{2,1,0:T(8,128)(2,1)S(1)}, u32[]{:S(2)}) copy-start(bf16[4,32,2048]{2,1,0:T(8,128)(2,1)S(1)} %collective-permute-done.53.refs_7_) | copy-start | bytes 1572868
  55.8 2.0 %collective-permute-start.55 = (bf16[4,32,2048]{2,1,0:T(8,128)(2,1)S(1)}, bf16[4,32,2048]{2,1,0:T(8,128)(2,1)}, u32[]{:S(2)}, u32[]{:S(2)}) collective-permute-start(bf16[4,32,2048]{2,1,0:T(8,128)(2,1)S(1)} %collective-permute-done.53.refs_7_), channel_id=1, source_target_pairs={{0,1},{1,0},{2,3},{3,2},{4,5},{5,4},{6,7},{7,6},{8,9},{9,8},{10,11... | collective-permute-start | bytes 1572872 | tf_op jit(solution)/shard_map/ppermute | solution.py:332
  56.9 0.9 copy-start.14
  56.9 1.1 copy-start.12
  90.5 16.2 %collective-permute-start.57 = (bf16[4,4,16,2176]{3,2,1,0:T(8,128)(2,1)}, bf16[4,4,16,2176]{3,2,1,0:T(8,128)(2,1)S(1)}, u32[]{:S(2)}, u32[]{:S(2)}) collective-permute-start(bf16[4,4,16,2176]{3,2,1,0:T(8,128)(2,1)} %get-tuple-element.135), channel_id=1, source_target_pairs={{0,1},{1,0},{2,3},{3,2},{4,5},{5,4},{6,7},{7,6},{8,9},{9,8},{10,11... | collective-permute-start | bytes 3342344 | tf_op jit(solution)/shard_map/ppermute | solution.py:332
  104.1 13.4 %collective-permute-start.56 = (bf16[2,3,16,8,512]{4,3,2,1,0:T(8,128)(2,1)}, bf16[2,3,16,8,512]{4,3,2,1,0:T(8,128)(2,1)S(1)}, u32[]{:S(2)}, u32[]{:S(2)}) collective-permute-start(bf16[2,3,16,8,512]{4,3,2,1,0:T(8,128)(2,1)} %get-tuple-element.131), channel_id=1, source_target_pairs={{0,1},{1,2},{2,3},{3,4},{4,5},{5,6},{6,7},{7,0},{8,9},{9,10},{10,1... | collective-permute-start | bytes 2359304 | tf_op jit(solution)/shard_map/ppermute | solution.py:289
  109.1 25.7 %copy-start = (bf16[2,3,16,8,512]{4,3,2,1,0:T(8,128)(2,1)S(1)}, bf16[2,3,16,8,512]{4,3,2,1,0:T(8,128)(2,1)}, u32[]{:S(2)}) copy-start(bf16[2,3,16,8,512]{4,3,2,1,0:T(8,128)(2,1)} %get-tuple-element.131) | copy-start | bytes 2359300
  109.1 11.8 %collective-permute-start.58 = (bf16[4,16,2176]{2,1,0:T(8,128)(2,1)}, bf16[4,16,2176]{2,1,0:T(8,128)(2,1)}, u32[]{:S(2)}, u32[]{:S(2)}) collective-permute-start(bf16[4,16,2176]{2,1,0:T(8,128)(2,1)} %get-tuple-element.147), channel_id=1, source_target_pairs={{0,8},{8,16},{16,24},{24,0},{1,9},{9,17},{17,25},{25,1},{2,10},{10... | collective-permute-start | bytes 835592 | tf_op jit(solution)/shard_map/ppermute | solution.py:332
  110.9 16.6 %collective-permute-start.60 = (bf16[4,16,2176]{2,1,0:T(8,128)(2,1)}, bf16[4,16,2176]{2,1,0:T(8,128)(2,1)}, u32[]{:S(2)}, u32[]{:S(2)}) collective-permute-start(bf16[4,16,2176]{2,1,0:T(8,128)(2,1)} %get-tuple-element.148), channel_id=1, source_target_pairs={{0,24},{8,0},{16,8},{24,16},{1,25},{9,1},{17,9},{25,17},{2,26},{10... | collective-permute-start | bytes 835592 | tf_op jit(solution)/shard_map/ppermute | solution.py:332
  113.1 14.5 %collective-permute-start.59 = (bf16[4,16,2176]{2,1,0:T(8,128)(2,1)S(1)}, bf16[4,16,2176]{2,1,0:T(8,128)(2,1)}, u32[]{:S(2)}, u32[]{:S(2)}) collective-permute-start(bf16[4,16,2176]{2,1,0:T(8,128)(2,1)S(1)} %get-tuple-element.149), channel_id=1, source_target_pairs={{0,16},{8,24},{16,0},{24,8},{1,17},{9,25},{17,1},{25,9},{2,18},{10... | collective-permute-start | bytes 835592 | tf_op jit(solution)/shard_map/ppermute | solution.py:332
  117.6 0.9 copy-start.1
  118.4 16.4 %copy-start.2 = (bf16[2,3,16,8,512]{4,3,2,1,0:T(8,128)(2,1)S(1)}, bf16[2,3,16,8,512]{4,3,2,1,0:T(8,128)(2,1)}, u32[]{:S(2)}) copy-start(bf16[2,3,16,8,512]{4,3,2,1,0:T(8,128)(2,1)} %copy-done.1) | copy-start | bytes 2359300
  118.4 49.5 %collective-permute-start.64 = (bf16[2,8,7,8,512]{4,3,2,1,0:T(8,128)(2,1)}, bf16[2,8,7,8,512]{4,3,2,1,0:T(8,128)(2,1)S(1)}, u32[]{:S(2)}, u32[]{:S(2)}) collective-permute-start(bf16[2,8,7,8,512]{4,3,2,1,0:T(8,128)(2,1)} %get-tuple-element.138), channel_id=1, source_target_pairs={{0,1},{1,2},{2,3},{3,4},{4,5},{5,6},{6,7},{7,0},{8,9},{9,10},{10,1... | collective-permute-start | bytes 2752520 | tf_op jit(solution)/shard_map/ppermute | solution.py:289
  129.5 38.4 %collective-permute-start.63 = (bf16[16,2176]{1,0:T(8,128)(2,1)}, bf16[16,2176]{1,0:T(8,128)(2,1)S(1)}, u32[]{:S(2)}, u32[]{:S(2)}) collective-permute-start(bf16[16,2176]{1,0:T(8,128)(2,1)} %get-tuple-element.154), channel_id=1, source_target_pairs={{0,6},{1,7},{2,0},{3,1},{4,2},{5,3},{6,4},{7,5},{8,14},{9,15},{10,... | collective-permute-start | bytes 208904 | tf_op jit(solution)/shard_map/ppermute | solution.py:332
  134.2 33.7 %collective-permute-start.62 = (bf16[16,2176]{1,0:T(8,128)(2,1)}, bf16[16,2176]{1,0:T(8,128)(2,1)S(1)}, u32[]{:S(2)}, u32[]{:S(2)}) collective-permute-start(bf16[16,2176]{1,0:T(8,128)(2,1)} %get-tuple-element.155), channel_id=1, source_target_pairs={{0,4},{1,5},{2,6},{3,7},{4,0},{5,1},{6,2},{7,3},{8,12},{9,13},{10,... | collective-permute-start | bytes 208904 | tf_op jit(solution)/shard_map/ppermute | solution.py:332
  134.2 33.7 %collective-permute-start.61 = (bf16[16,2176]{1,0:T(8,128)(2,1)}, bf16[16,2176]{1,0:T(8,128)(2,1)S(1)}, u32[]{:S(2)}, u32[]{:S(2)}) collective-permute-start(bf16[16,2176]{1,0:T(8,128)(2,1)} %get-tuple-element.156), channel_id=1, source_target_pairs={{0,2},{1,3},{2,4},{3,5},{4,6},{5,7},{6,0},{7,1},{8,10},{9,11},{10,... | collective-permute-start | bytes 208904 | tf_op jit(solution)/shard_map/ppermute | solution.py:332
  135.0 36.0 %copy-start.3 = (bf16[8,16,8,512]{3,2,1,0:T(8,128)(2,1)S(1)}, bf16[8,16,8,512]{3,2,1,0:T(8,128)(2,1)}, u32[]{:S(2)}) copy-start(bf16[8,16,8,512]{3,2,1,0:T(8,128)(2,1)} %get-tuple-element.130) | copy-start | bytes 3145732
  135.0 36.0 %copy-start.5 = (bf16[8,16,8,512]{3,2,1,0:T(8,128)(2,1)S(1)}, bf16[8,16,8,512]{3,2,1,0:T(8,128)(2,1)}, u32[]{:S(2)}) copy-start(bf16[8,16,8,512]{3,2,1,0:T(8,128)(2,1)} %get-tuple-element.141) | copy-start | bytes 3145732
  135.1 31.9 %collective-permute-start.36 = (bf16[2,2,16,8,512]{4,3,2,1,0:T(8,128)(2,1)S(1)}, bf16[2,2,16,8,512]{4,3,2,1,0:T(8,128)(2,1)S(1)}, u32[]{:S(2)}, u32[]{:S(2)}) collective-permute-start(bf16[2,2,16,8,512]{4,3,2,1,0:T(8,128)(2,1)S(1)} %slice.149), channel_id=1, source_target_pairs={{0,8},{1,9},{2,10},{3,11},{4,12},{5,13},{6,14},{7,15},{8,16},{9,17... | collective-permute-start | bytes 1572872 | tf_op jit(solution)/shard_map/cond/branch_12_fun/ppermute | solution.py:289
  168.0 5.9 %collective-permute-start.67 = (bf16[16,2176]{1,0:T(8,128)(2,1)S(1)}, bf16[16,2176]{1,0:T(8,128)(2,1)S(1)}, u32[]{:S(2)}, u32[]{:S(2)}) collective-permute-start(bf16[16,2176]{1,0:T(8,128)(2,1)S(1)} %get-tuple-element.146), channel_id=1, source_target_pairs={{0,8},{8,16},{16,24},{24,0},{1,9},{9,17},{17,25},{25,1},{2,10},{10... | collective-permute-start | bytes 208904 | tf_op jit(solution)/shard_map/ppermute | solution.py:332
  168.0 5.8 %collective-permute-start.66 = (bf16[16,2176]{1,0:T(8,128)(2,1)S(1)}, bf16[16,2176]{1,0:T(8,128)(2,1)S(1)}, u32[]{:S(2)}, u32[]{:S(2)}) collective-permute-start(bf16[16,2176]{1,0:T(8,128)(2,1)S(1)} %get-tuple-element.146), channel_id=1, source_target_pairs={{0,16},{8,24},{16,0},{24,8},{1,17},{9,25},{17,1},{25,9},{2,18},{10... | collective-permute-start | bytes 208904 | tf_op jit(solution)/shard_map/ppermute | solution.py:332
  168.1 5.7 %collective-permute-start.65 = (bf16[16,2176]{1,0:T(8,128)(2,1)S(1)}, bf16[16,2176]{1,0:T(8,128)(2,1)S(1)}, u32[]{:S(2)}, u32[]{:S(2)}) collective-permute-start(bf16[16,2176]{1,0:T(8,128)(2,1)S(1)} %get-tuple-element.146), channel_id=1, source_target_pairs={{0,24},{8,0},{16,8},{24,16},{1,25},{9,1},{17,9},{25,17},{2,26},{10... | collective-permute-start | bytes 208904 | tf_op jit(solution)/shard_map/ppermute | solution.py:332
  172.9 1.2 copy-start.4
  172.9 1.3 copy-start.6
